TPU v7x, 256 devices: a whole 4x4x8 slice. The times are simulated.
256 devices in a mesh: sub: 64 (over z, x, core), blk: 4 (over y).
Axes of the slice: x: 4, y: 4, z: 8, core: 2. Of those that a mesh axis runs over, the one named last changes fastest.
Arguments:
- a_tiles: bfloat16 [6144, 12, 128, 128], P(('sub', 'blk'))
- modes: bfloat16 [6144, 16, 128], P(('sub', 'blk')), may hold values from -6 to 6
- col_tiles: int32 [6144, 12], P(('sub', 'blk')), may hold values from 0 to 225, as said below
- fetch_list: int32 [256, 130], P(('sub', 'blk')), may hold values from 0 to 6143, as said below
Outputs:
- prolong: bfloat16 [6144, 12, 16, 128], P(('sub', 'blk'))
- coarse_diag: float32 [6144, 256], P('sub')
Inputs may be any that keep to these rules, and one draw needn't show every extreme that they name: `col_tiles`: slot 0 of row tile t names t itself (its index within its group); the other slots name other tiles of the same group (values below 96) or 96 + h for entry h of the device's fetch list; every entry of a device's fetch list is named by some slot of that device's rows. `fetch_list`: A device's list is 26 blocks of 5 entries; each block names distinct tiles of one group other than the device's own, different blocks name different groups; tile i of group g has number g * 96 + i.
All inputs are finite; a program needn't handle non-finite values.
Results may differ from a plain program's by a relative error of at most 0.008.
Values may be sent and summed in bfloat16 or wider, within the bound.
A program may use at most 64 MiB of HBM per device.

v0:
```python
import jax
import jax.numpy as jnp
from jax import lax
from jax.sharding import PartitionSpec as P

NEIGHBOURS = 26


damping = 2.0 / 3.0


def sent_to_all(shard, axis):
    copies = jnp.broadcast_to(shard, (lax.axis_size(axis), *shard.shape))
    return lax.all_to_all(copies, axis, split_axis=0, concat_axis=0, tiled=True)


def of_everyone(shard, axis):
    everything = sent_to_all(shard, axis)
    return jnp.sum(everything.astype(jnp.float32), axis=0)


def shards(a_tiles, modes, col_tiles, fetch_list):
    blk_count = lax.axis_size("blk")
    sub_count = lax.axis_size("sub")
    tile_dev = a_tiles.shape[0]
    slot_count = a_tiles.shape[1]
    tile_rows = a_tiles.shape[2]
    mode_count = modes.shape[1]
    group_size = tile_dev * blk_count
    ghost_count = fetch_list.shape[1]
    peer_count = min(NEIGHBOURS, sub_count - 1)
    per_peer = ghost_count // peer_count
    group_modes = lax.all_gather(modes, "blk", axis=0, tiled=True)
    wanted = fetch_list[0].reshape(peer_count, per_peer)
    owners = wanted[:, 0] // group_size
    within = wanted % group_size
    selector = (owners[:, None] == jnp.arange(sub_count, dtype=jnp.int32)[None, :]).astype(
        jnp.int32
    )
    requests = jnp.sum(selector[:, :, None] * (within + 1)[:, None, :], axis=0)
    received = lax.all_to_all(requests, "sub", split_axis=0, concat_axis=0, tiled=True)
    present = received > 0
    picked = group_modes[jnp.maximum(received - 1, 0)]
    picked = jnp.where(present[:, :, None, None], picked, jnp.zeros_like(picked))
    returned = lax.all_to_all(picked, "sub", split_axis=0, concat_axis=0, tiled=True)
    returned, received = (returned, received)
    ghosts = returned[owners].reshape(ghost_count, mode_count, tile_rows)
    lookup = jnp.concatenate([group_modes, ghosts], axis=0)
    gathered = lookup[col_tiles]
    product = jnp.einsum("tkrc,tkmc->tkmr", a_tiles, gathered, preferred_element_type=jnp.float32)
    inverse = 1.0 / jnp.diagonal(a_tiles[:, 0], axis1=1, axis2=2).astype(jnp.float32)
    leading = (jnp.arange(slot_count) == 0).astype(jnp.float32)
    prolong = (
        leading[None, :, None, None] * modes.astype(jnp.float32)[:, None]
        - damping * inverse[:, None, None, :] * product
    ).astype(jnp.bfloat16)
    partial_value = (
        jnp.einsum(
            "tkmr,tknr->tkmn", prolong.astype(jnp.float32), product, precision=lax.Precision.HIGHEST
        )
        / tile_rows
    )
    partial_value = partial_value.reshape(tile_dev * slot_count, mode_count * mode_count)
    segment = (
        col_tiles.reshape(-1)[:, None]
        == jnp.arange(group_size + ghost_count, dtype=jnp.int32)[None, :]
    ).astype(jnp.float32)
    slot_sums = jnp.dot(
        segment.T,
        partial_value,
        precision=lax.Precision.HIGHEST,
        preferred_element_type=jnp.float32,
    )
    ghost_sums = slot_sums[group_size:].reshape(peer_count, per_peer, mode_count * mode_count)
    outgoing = jnp.einsum(
        "jp,jmv->pmv", selector.astype(jnp.float32), ghost_sums, precision=lax.Precision.HIGHEST
    )
    incoming = lax.all_to_all(
        outgoing.astype(jnp.bfloat16), "sub", split_axis=0, concat_axis=0, tiled=True
    ).astype(outgoing.dtype)
    target = (
        received[:, :, None] == jnp.arange(1, group_size + 1, dtype=jnp.int32)[None, None, :]
    ).astype(jnp.float32)
    local_sum = slot_sums[:group_size] + jnp.einsum(
        "pmg,pmv->gv", target, incoming, precision=lax.Precision.HIGHEST
    )
    coarse_diag = of_everyone(local_sum.astype(jnp.bfloat16), "blk").astype(jnp.float32)
    return (prolong, coarse_diag)


def solution(mesh):
    in_specs = (
        P(("sub", "blk"), None, None, None),
        P(("sub", "blk"), None, None),
        P(("sub", "blk"), None),
        P(("sub", "blk"), None),
    )
    out_specs = (P(("sub", "blk"), None, None, None), P("sub", None))
    return jax.shard_map(shards, mesh=mesh, in_specs=in_specs, out_specs=out_specs, check_vma=False)
```

profile of v0, /device:TPU:1, one launch (start us, length us, event | category | flops | bytes accessed | tf_op | source)
XLA Modules:
  0.0 123.1 jit_solution(14701168160564173144)
XLA Ops:
  0.6 0.5 broadcast.171
  1.1 1.3 %reduce.10 = s32[130]{0:T(256)S(1)} reduce(s32[1,130]{1,0:T(1,128)} %param.7, s32[]{:T(128)} %broadcast.171), dimensions={0}, to_apply=%param.7.reduce_sub_computation.3 | reduce | bytes 1044 | tf_op args[3]
  2.7 0.1 fusion.9
  2.9 0.1 multiply_reduce_fusion
  3.0 0.7 copy.42
  3.7 13.0 %all-to-all-start = ((s32[64,1,5]{2,1,0:T(1,128)}), s32[64,1,5]{2,1,0:T(1,128)S(1)}, u32[]{:S(2)}, u32[]{:S(2)}) async-start(s32[64,1,5]{2,1,0:T(1,128)} %copy.42), calls=%async_computation | async-start | bytes 65536 | tf_op jit(solution)/shard_map/all_to_all | solution.py:41
  16.7 11.2 %all_gather.3 = bf16[96,16,128]{2,1,0:T(8,128)(2,1)S(1)} all-gather(bf16[24,16,128]{2,1,0:T(8,128)(2,1)} %param.5), channel_id=1, replica_groups=mesh['sub'=64,'blk'=4] {'blk'}, dimensions={0}, use_global_device_ids=true | all-gather | bytes 491520 | tf_op jit(solution)/shard_map/all_gather | solution.py:33
  27.9 0.1 maximum_reduce_fusion
  28.0 0.1 reshape.101
  28.2 1.9 %gather_fusion.1 = bf16[320,16,128]{2,1,0:T(8,128)(2,1)S(1)} fusion(bf16[96,16,128]{2,1,0:T(8,128)(2,1)S(1)} %all_gather.3, s32[1024]{0:T(1024)S(1)} %pad_clamp_fusion.2), kind=kCustom, calls=%fused_computation.1 | custom fusion | bytes 2622720 | tf_op jit(solution)/shard_map/gather | solution.py:43
  30.0 1.4 %broadcast_select_fusion = bf16[64,5,16,128]{3,2,1,0:T(8,128)(2,1)} fusion(bf16[64,5,16,128]{3,2,1,0:T(8,128)(2,1)S(1)} %bitcast.26, pred[64,5]{1,0:T(8,128)(4,1)S(1)} %broadcast_compare_fusion), kind=kLoop, calls=%fused_computation.6 | loop fusion | flops 655360 | bytes 2621760 | tf_op jit(solution)/shard_map/jit(_where)/select_n | solution.py:44
  31.4 12.5 %all-to-all-start.1 = ((bf16[64,5,16,128]{3,2,1,0:T(8,128)(2,1)}), bf16[64,5,16,128]{3,2,1,0:T(8,128)(2,1)S(1)}, u32[]{:S(2)}, u32[]{:S(2)}) async-start(bf16[64,5,16,128]{3,2,1,0:T(8,128)(2,1)} %broadcast_select_fusion), calls=%async_computation.1 | async-start | bytes 2621440 | tf_op jit(solution)/shard_map/all_to_all | solution.py:45
  44.0 1.1 slice-done
  45.1 3.2 %copy.49 = bf16[24,1,128,128]{0,3,2,1:T(8,128)(2,1)} copy(bf16[24,1,128,128]{3,2,1,0:T(8,128)(2,1)S(1)} %slice-done) | data formatting | bytes 1572864
  48.3 1.9 %gather_fusion = bf16[128,24]{1,0:T(8,128)(2,1)S(1)} fusion(bf16[24,128,128]{0,2,1:T(8,128)(2,1)} %bitcast.28, s32[128]{0:T(128)S(1)} %or_bitcast_fusion), kind=kCustom, calls=%fused_computation | custom fusion | bytes 13312 | tf_op jit(solution)/shard_map/jit(diagonal)/gather | solution.py:51
  50.3 0.1 copy.44
  50.5 0.1 reshape.117
  50.7 26.8 %all-to-all-done.1 = bf16[64,5,16,128]{3,2,1,0:T(8,128)(2,1)S(1)} async-done(((bf16[64,5,16,128]{3,2,1,0:T(8,128)(2,1)}), bf16[64,5,16,128]{3,2,1,0:T(8,128)(2,1)S(1)}, u32[]{:S(2)}, u32[]{:S(2)}) %all-to-all-start.1) | async-done | bytes 1310752 | tf_op jit(solution)/shard_map/all_to_all | solution.py:45
  77.5 0.6 gather_fusion.2
  78.3 1.8 %gather_fusion.3 = bf16[288,16,128]{2,1,0:T(8,128)(2,1)S(1)} fusion(bf16[226,16,128]{2,1,0:T(8,128)(2,1)S(1)} %pad_maximum_fusion, s32[1024]{0:T(1024)S(1)} %pad_clamp_fusion), kind=kCustom, calls=%fused_computation.3 | custom fusion | bytes 2360448 | tf_op jit(solution)/shard_map/gather | solution.py:49
  80.1 7.5 %subtract_convert_fusion = (bf16[24,12,16,128]{3,2,1,0:T(8,128)(2,1)S(1)}, f32[24,12,16,128]{3,2,1,0:T(8,128)S(1)}) fusion(f32[24,128]{1,0:T(8,128)S(1)} %multiply_bitcast_fusion, f32[24,16,128]{2,1,0:T(8,128)S(1)} %convert_element_type.44, f32[12]{0:T(128)S(1)} %compare_convert_fusion, bf16[24,12,16,128]{3,2,1,0:T(8,128)(2,1)S(1)} %bitcast.27, ...), kind=kOutput, calls=%fused_computation.4 | convolution fusion | flops 153354240 | bytes 14364720 | tf_op jit(solution)/shard_map/tkrc,tkmc->tkmr/dot_general | solution.py:50
  87.6 1.0 copy-done
  88.6 1.9 %convolution_multiply_fusion = f32[24,12,16,16]{3,2,1,0:T(8,128)S(1)} fusion(bf16[24,12,16,128]{3,2,1,0:T(8,128)(2,1)S(1)} %get-tuple-element.4, f32[24,12,16,128]{3,2,1,0:T(8,128)S(1)} %get-tuple-element.5), kind=kOutput, calls=%fused_computation.5 | convolution fusion | flops 113319936 | bytes 3833856 | tf_op jit(solution)/shard_map/tkmr,tknr->tkmn/dot_general | solution.py:58
  90.6 1.1 reshape.91
  91.6 0.6 fusion.2
  92.3 0.5 convolution_convert_fusion
  92.8 0.8 copy.47
  93.6 6.3 %all-to-all-start.2 = ((bf16[64,5,256]{2,1,0:T(8,128)(2,1)}), bf16[64,5,256]{2,1,0:T(8,128)(2,1)S(1)}, u32[]{:S(2)}, u32[]{:S(2)}) async-start(bf16[64,5,256]{2,1,0:T(8,128)(2,1)} %copy.47), calls=%async_computation.2 | async-start | bytes 524288 | tf_op jit(solution)/shard_map/all_to_all | solution.py:78
  100.0 13.1 %all-to-all-done.2 = bf16[64,5,256]{2,1,0:T(8,128)(2,1)S(1)} async-done(((bf16[64,5,256]{2,1,0:T(8,128)(2,1)}), bf16[64,5,256]{2,1,0:T(8,128)(2,1)S(1)}, u32[]{:S(2)}, u32[]{:S(2)}) %all-to-all-start.2) | async-done | bytes 163872 | tf_op jit(solution)/shard_map/all_to_all | solution.py:78
  113.1 0.3 fusion.1
  113.4 8.9 %all_to_all.27 = bf16[4,96,256]{2,1,0:T(8,128)(2,1)S(1)} all-to-all(bf16[4,96,256]{2,1,0:T(8,128)(2,1)S(1)} %broadcast_in_dim.21), channel_id=1, replica_groups=mesh['sub'=64,'blk'=4] {'blk'}, dimensions={0} | all-to-all | bytes 393216 | tf_op jit(solution)/shard_map/all_to_all | solution.py:14
  122.4 0.7 convert_reduce_fusion
  (29 shorter events, 0.8 us)
Async XLA Ops:
  3.7 24.2 %all-to-all-start = ((s32[64,1,5]{2,1,0:T(1,128)}), s32[64,1,5]{2,1,0:T(1,128)S(1)}, u32[]{:S(2)}, u32[]{:S(2)}) async-start(s32[64,1,5]{2,1,0:T(1,128)} %copy.42), calls=%async_computation | async-start | bytes 65536 | tf_op jit(solution)/shard_map/all_to_all | solution.py:41
  31.4 12.5 %copy-start.1 = (bf16[24,16,128]{2,1,0:T(8,128)(2,1)S(1)}, bf16[24,16,128]{2,1,0:T(8,128)(2,1)}, u32[]{:S(2)}) copy-start(bf16[24,16,128]{2,1,0:T(8,128)(2,1)} %param.5) | copy-start | bytes 294916
  31.4 46.1 %all-to-all-start.1 = ((bf16[64,5,16,128]{3,2,1,0:T(8,128)(2,1)}), bf16[64,5,16,128]{3,2,1,0:T(8,128)(2,1)S(1)}, u32[]{:S(2)}, u32[]{:S(2)}) async-start(bf16[64,5,16,128]{3,2,1,0:T(8,128)(2,1)} %broadcast_select_fusion), calls=%async_computation.1 | async-start | bytes 2621440 | tf_op jit(solution)/shard_map/all_to_all | solution.py:45
  43.9 1.1 slice-start
  45.1 5.2 %copy-start.2 = (s32[24,12]{0,1:T(8,128)S(1)}, s32[24,12]{0,1:T(8,128)}, u32[]{:S(2)}) copy-start(s32[24,12]{0,1:T(8,128)} %param.6) | copy-start | bytes 3460
  87.6 1.0 copy-start
  93.6 19.5 %all-to-all-start.2 = ((bf16[64,5,256]{2,1,0:T(8,128)(2,1)}), bf16[64,5,256]{2,1,0:T(8,128)(2,1)S(1)}, u32[]{:S(2)}, u32[]{:S(2)}) async-start(bf16[64,5,256]{2,1,0:T(8,128)(2,1)} %copy.47), calls=%async_computation.2 | async-start | bytes 524288 | tf_op jit(solution)/shard_map/all_to_all | solution.py:78
where the time goes:
time: 123 us
  waiting for transfers between devices  39.9 us (32%)
  starting transfers between devices  31.8 us (26%)
  blocking collectives  20.1 us (16%)
  local copies, waits for them, and re-layouts  15.6 us (13%)
  matrix products  10.9 us (9%)
  other arithmetic  3.94 us (3%)
    all_to_all x1, waiting for transfers between devices, shards(): lax.all_to_all(picked, 'sub', split_axis=0, concat_axis=0, tiled=True)  26.8 us
    all_to_all x1, waiting for transfers between devices, shards(): lax.all_to_all(outgoing.astype(jnp.bfloat16), 'sub', split_axis=0, concat...  13.1 us
    all_to_all x1, starting transfers between devices, shards(): lax.all_to_all(requests, 'sub', split_axis=0, concat_axis=0, tiled=True)  13 us
    all_to_all x1, starting transfers between devices, shards(): lax.all_to_all(picked, 'sub', split_axis=0, concat_axis=0, tiled=True)  12.5 us
    all_gather x1, blocking collectives, shards(): group_modes = lax.all_gather(modes, 'blk', axis=0, tiled=True)  11.2 us
    all_to_all x1, blocking collectives, sent_to_all(): return lax.all_to_all(copies, axis, split_axis=0, concat_axis=0, tiled=True)  8.94 us
    dot_general x1, matrix products, shards(): jnp.einsum('tkrc,tkmc->tkmr', a_tiles, gathered, preferred_element_type=j...  7.47 us
    all_to_all x1, starting transfers between devices, shards(): lax.all_to_all(outgoing.astype(jnp.bfloat16), 'sub', split_axis=0, concat...  6.33 us
  transfers between devices with their start and end apart: 3, of which 2 were waited for; matrix products, arithmetic and copies ran while one was open for 5% of the time, Pallas kernels for 0%

commit v1 on v0

v1 whole, which is shorter than its diff:
```python
import functools

import jax
import jax.numpy as jnp
from jax import lax
from jax.experimental import pallas as pl
from jax.experimental.pallas import tpu as pltpu
from jax.sharding import PartitionSpec as P

MESH = pl.DeviceIdType.MESH
BF = jnp.bfloat16
F32 = jnp.float32
NZ, NX, NC, NY = 8, 4, 2, 4
TILE_DEV = 24
SLOTS = 12
SLOTP = 16
ROWS = 128
MODES = 16
GROUP = 96
GROUPS = NZ * NX * NC
TILES = GROUP * GROUPS
PER_PEER = 5
GHOSTS = 130
GHOSTP = 144
LIST = 256
NQ = 2
XQ = NX // NQ
OUT_ROWS = GROUP + GROUPS * 8
DAMPING = 2.0 / 3.0


def dev(z, x, c, y):
    return ((z * NX + x) * NC + c, y)


def rcopy(src, dst, send, recv, device):
    return pltpu.make_async_remote_copy(
        src_ref=src, dst_ref=dst, send_sem=send, recv_sem=recv, device_id=device, device_id_type=MESH
    )


def dot_t(a, b):
    return lax.dot_general(a, b, (((1,), (1,)), ((), ())), preferred_element_type=F32)


def body(
    modes, fetch_v, fetch_s, col_s, col_v, a_hbm, prolong, coarse,
    a_v, mf, s1, blocks, rows_f, lists_v, lists_s, stage, msg, got, got_f, table,
    pv, qv, flat, seg, req, idx1, idx2, target, out, in1, in2, ysum,
    a_sem, scat_s, scat_r, list_s, list_r, own_sem, all_s, all_r, ring_s, ring_r, sib_s, sib_r,
    ex_s, ex_r, id1_s, id1_r, id2_s, id2_r, c1_s, c1_r, c2_s, c2_r, y_s, y_r, p_sem,
):
    s = lax.axis_index("sub")
    y = lax.axis_index("blk")
    z, x, c = s // (NX * NC), lax.rem(s // NC, NX), lax.rem(s, NC)
    me = x * NY + y
    xc = x * NC + c
    right, left = dev(lax.rem(z + 1, NZ), x, c, y), dev(lax.rem(z + NZ - 1, NZ), x, c, y)
    sibling = dev(z, x, 1 - c, y)

    def plane(p):
        tx, ty = lax.rem(x + p // NY, NX), lax.rem(y + p % NY, NY)
        return tx * NY + ty, dev(z, tx, c, ty)

    def along_z(d):
        tz = lax.rem(z + d, NZ)
        return tz, dev(tz, x, c, y)

    def across(d):
        t = lax.rem(xc + d, NX * NC)
        return t, (z * NX * NC + t, y)

    def along_y(d):
        return dev(z, x, c, lax.rem(y + d, NY))

    for t in range(TILE_DEV):
        pltpu.make_async_copy(a_hbm.at[t], a_v.at[t], a_sem.at[t]).start()

    barrier = pltpu.get_barrier_semaphore()
    partners = [plane(p)[1] for p in range(1, NX * NY)]
    partners += [along_z(d)[1] for d in range(1, NZ)]
    partners += [dev(z, lax.rem(x + d, NX), 1 - c, y) for d in range(NX)]
    for partner in partners:
        pl.semaphore_signal(barrier, inc=1, device_id=partner, device_id_type=MESH)

    mf[...] = modes[...].astype(F32).reshape(TILE_DEV * MODES, ROWS)
    for m in range(MODES):
        s1[m] = mf[pl.ds(m, TILE_DEV, stride=MODES), :].astype(BF)

    lane = lax.broadcasted_iota(jnp.int32, (8, 128), 1)
    sub8 = lax.broadcasted_iota(jnp.int32, (8, 128), 0)
    request = jnp.full((8, 128), -1, jnp.int32)
    slots = col_v[...]
    colvec = slots
    for h in range(GHOSTS):
        tile = fetch_s[0, h]
        group = tile // GROUP
        request = jnp.where(
            (lane == group) & (sub8 == h % PER_PEER), tile - group * GROUP, request
        )
        slots = jnp.where(colvec == GROUP + h, GROUP + group * 8 + h % PER_PEER, slots)
    req[...] = request

    pl.semaphore_wait(barrier, len(partners))

    pltpu.make_async_copy(s1.at[me], blocks.at[z, c, x, y], scat_r.at[x]).start()
    for p in range(1, NX * NY):
        t, device = plane(p)
        rcopy(s1.at[t], blocks.at[z, c, x, y], scat_s.at[0], scat_r.at[x], device).start()
    pltpu.make_async_copy(fetch_v, lists_v.at[me], own_sem.at[0]).start()
    for p in range(1, NX * NY):
        rcopy(fetch_v, lists_v.at[me], list_s.at[0], list_r.at[0], plane(p)[1]).start()
    for d in range(1, NZ):
        rcopy(req, idx1.at[z], id1_s.at[0], id1_r.at[0], along_z(d)[1]).start()
    mine = table.at[pl.ds(y * TILE_DEV, TILE_DEV)]
    pltpu.make_async_copy(modes, mine, own_sem.at[1]).start()
    for d in range(1, NY):
        rcopy(modes, mine, all_s.at[0], all_r.at[0], along_y(d)).start()
    idx1[z] = request

    def piece(k, core, q):
        return blocks.at[k, core, pl.ds(q * XQ, XQ)]

    def ring(way, step, q, k):
        part = piece(k, c, q)
        device = right if way == 0 else left
        rcopy(part, part, ring_s.at[0], ring_r.at[way, step, q], device).start()

    def pass_on(way, step, q, k):
        part = piece(k, c, q)
        rcopy(part, part, sib_s.at[0], sib_r.at[way, step, q], sibling).start()

    def widen(k, core, q):
        @pl.loop(0, XQ * NY)
        def _(i):
            xs, ys = q * XQ + i // NY, lax.rem(i, NY)
            base = ((k * NX + xs) * NC + core) * GROUP + ys * TILE_DEV
            rows_f[pl.ds(pl.multiple_of(base, 8), TILE_DEV), :] = blocks[k, core, xs, ys].astype(F32)

    def from_sibling(way, step, q, k):
        part = piece(k, 1 - c, q)
        rcopy(part, part, sib_s.at[0], sib_r.at[way, step, q], sibling).wait_recv()
        widen(k, 1 - c, q)

    last = NZ // 2
    for q in range(NQ):
        for xs in range(q * XQ, (q + 1) * XQ):
            part = blocks.at[z, c, xs]
            rcopy(part, part, scat_s.at[0], scat_r.at[xs], sibling).wait_recv()
        ring(0, 0, q, z)
        ring(1, 0, q, z)
        pass_on(0, 0, q, z)

    pltpu.make_async_copy(fetch_v, lists_v.at[me], own_sem.at[0]).wait()
    others = lists_v.at[pl.ds(0, NX * NY - 1)]
    rcopy(others, others, list_s.at[0], list_r.at[0], sibling).wait_recv()
    pltpu.make_async_copy(lists_v, lists_s, own_sem.at[2]).start()
    others = idx1.at[pl.ds(0, NZ - 1)]
    rcopy(others, others, id1_s.at[0], id1_r.at[0], sibling).wait_recv()
    for d in range(1, NX * NC):
        rcopy(idx1, idx2.at[xc], id2_s.at[0], id2_r.at[0], across(d)[1]).start()
    idx2[xc] = idx1[...]
    for q in range(NQ):
        widen(z, c, q)

    events = []
    for step in range(1, last + 1):
        for q in range(NQ):
            for way in range(2):
                if step < last or q == way:
                    events.append((way, step, q))
    pending = [(0, 0, q, z) for q in range(NQ)]
    for way, step, q in events:
        k = lax.rem(z + NZ - step, NZ) if way == 0 else lax.rem(z + step, NZ)
        part = piece(k, c, q)
        rcopy(part, part, ring_s.at[0], ring_r.at[way, step - 1, q], sibling).wait_recv()
        if step < last - 1 or (step == last - 1 and q == way):
            ring(way, step, q, k)
        pass_on(way, step, q, k)
        widen(k, c, q)
        pending.append((way, step, q, k))
        if len(pending) > 3:
            from_sibling(*pending.pop(0))
    pltpu.make_async_copy(lists_v, lists_s, own_sem.at[2]).wait()
    for item in pending:
        from_sibling(*item)

    def pick(t):
        for h in range(GHOSTS):
            stage[pl.ds(h, 1), :] = rows_f[pl.ds(lists_s[t, 0, h], 1), :]
        return stage[...].astype(BF)

    stage[pl.ds(GHOSTS - 2, GHOSTP - GHOSTS + 2), :] = jnp.zeros((GHOSTP - GHOSTS + 2, ROWS), F32)

    @pl.loop(1, NX * NY)
    def _(p):
        tx, ty = lax.rem(x + p // NY, NX), lax.rem(y + lax.rem(p, NY), NY)
        t = tx * NY + ty
        msg[t] = pick(t)
        rcopy(msg.at[t], got.at[me], ex_s.at[0], ex_r.at[0], dev(z, tx, c, ty)).start()

    got[me] = pick(me)

    place = lax.broadcasted_iota(jnp.int32, (OUT_ROWS, TILE_DEV * SLOTP), 0)
    seg[...] = (place == slots).astype(F32).astype(BF)
    others = idx2.at[pl.ds(0, NX * NC - 1)]
    rcopy(others, others, id2_s.at[0], id2_r.at[0], sibling).wait_recv()
    wanted = idx2[...].reshape(GROUPS * 8, 128)
    lanes = lax.broadcasted_iota(jnp.int32, (GROUPS * 8, 128), 1)
    chosen = jnp.sum(jnp.where(lanes == s, wanted, 0).astype(F32), axis=1, keepdims=True)
    target[...] = (lanes.astype(F32) == chosen).astype(F32).T.astype(BF)

    pltpu.make_async_copy(modes, mine, own_sem.at[1]).wait()
    others = table.at[pl.ds(0, (NY - 1) * TILE_DEV)]
    rcopy(others, others, all_s.at[0], all_r.at[0], sibling).wait_recv()
    others = got.at[pl.ds(0, NX * NY - 1)]
    rcopy(others, others, ex_s.at[0], ex_r.at[0], sibling).wait_recv()
    for m in range(MODES):
        got_f[pl.ds(m * GHOSTP, GHOSTP), :] = got[m].astype(F32)
    for h in range(GHOSTS):
        table[GROUP + h] = got_f[pl.ds(h, MODES, stride=GHOSTP), :].astype(BF)

    eye = lax.broadcasted_iota(jnp.int32, (ROWS, ROWS), 0) == lax.broadcasted_iota(
        jnp.int32, (ROWS, ROWS), 1
    )
    n = SLOTS * MODES
    same_slot = (
        lax.broadcasted_iota(jnp.int32, (n, n), 0) // MODES
        == lax.broadcasted_iota(jnp.int32, (n, n), 1) // MODES
    )
    spread = (
        lax.rem(lax.broadcasted_iota(jnp.int32, (n, MODES * MODES), 0), MODES)
        == lax.rem(lax.broadcasted_iota(jnp.int32, (n, MODES * MODES), 1), MODES)
    ).astype(F32).astype(BF)
    same_mode = (
        lax.rem(lax.broadcasted_iota(jnp.int32, (n, MODES * MODES), 0), MODES)
        == lax.broadcasted_iota(jnp.int32, (n, MODES * MODES), 1) // MODES
    )
    fold = (
        lax.broadcasted_iota(jnp.int32, (SLOTP, n), 0)
        == lax.broadcasted_iota(jnp.int32, (SLOTP, n), 1) // MODES
    ).astype(F32).astype(BF)

    @pl.loop(0, TILE_DEV)
    def _(t):
        pltpu.make_async_copy(a_hbm.at[t], a_v.at[t], a_sem.at[t]).wait()
        diagonal = jnp.sum(jnp.where(eye, a_v[t, 0].astype(F32), 0.0), axis=0, keepdims=True)
        scale = DAMPING / diagonal
        for k in range(SLOTS):
            column = table[col_s[0, t * SLOTP + k]]
            product = dot_t(column, a_v[t, k])
            value = -scale * product
            if k == 0:
                value = modes[t].astype(F32) + value
            pv[t, k] = value.astype(BF)
            qv[k] = product.astype(BF)
        both = dot_t(pv[t].reshape(n, ROWS), qv[...].reshape(n, ROWS)) * (1.0 / ROWS)
        both = jnp.where(same_slot, both, 0.0).astype(BF)
        wide = jnp.dot(both, spread, preferred_element_type=F32)
        wide = jnp.where(same_mode, wide, 0.0).astype(BF)
        flat[pl.ds(pl.multiple_of(t * SLOTP, SLOTP), SLOTP), :] = jnp.dot(
            fold, wide, preferred_element_type=F32
        ).astype(BF)

    pltpu.make_async_copy(pv, prolong, p_sem.at[0]).start()

    sums = jnp.dot(seg[...], flat[...], preferred_element_type=F32)
    out[...] = sums[GROUP:].astype(BF).reshape(NZ, NX * NC, 8, MODES * MODES)
    for d in range(1, NZ):
        tz, device = along_z(d)
        rcopy(out.at[tz], in1.at[z], c1_s.at[0], c1_r.at[0], device).start()
    in1[z] = out[z]
    others = in1.at[pl.ds(0, NZ - 1)]
    rcopy(others, others, c1_s.at[0], c1_r.at[0], sibling).wait_recv()
    for d in range(1, NX * NC):
        t, device = across(d)
        rcopy(in1.at[:, t], in2.at[xc], c2_s.at[0], c2_r.at[0], device).start()
    in2[xc] = in1[:, xc]
    others = in2.at[pl.ds(0, NX * NC - 1)]
    rcopy(others, others, c2_s.at[0], c2_r.at[0], sibling).wait_recv()
    returned = jnp.dot(
        target[...], in2[...].reshape(GROUPS * 8, MODES * MODES), preferred_element_type=F32
    )
    ysum[y] = (sums[:GROUP] + returned[:GROUP]).astype(BF)
    for d in range(1, NY):
        rcopy(ysum.at[y], ysum.at[y], y_s.at[0], y_r.at[0], along_y(d)).start()
    others = ysum.at[pl.ds(0, NY - 1)]
    rcopy(others, others, y_s.at[0], y_r.at[0], sibling).wait_recv()
    total = ysum[0].astype(F32)
    for k in range(1, NY):
        total = total + ysum[k].astype(F32)
    coarse[...] = total

    def sent(region, sem):
        rcopy(region, region, sem, sem, sibling).wait_send()

    sent(s1.at[pl.ds(0, NX * NY - 1)], scat_s.at[0])
    sent(lists_v.at[pl.ds(0, NX * NY - 1)], list_s.at[0])
    sent(idx1.at[pl.ds(0, NZ - 1)], id1_s.at[0])
    sent(idx2.at[pl.ds(0, NX * NC - 1)], id2_s.at[0])
    sent(table.at[pl.ds(0, (NY - 1) * TILE_DEV)], all_s.at[0])
    sent(blocks.at[pl.ds(0, NZ - 1), c], ring_s.at[0])
    sent(blocks.at[:, c], sib_s.at[0])
    sent(msg.at[pl.ds(0, NX * NY - 1)], ex_s.at[0])
    sent(out.at[pl.ds(0, NZ - 1)], c1_s.at[0])
    sent(in2.at[pl.ds(0, NX * NC - 1)], c2_s.at[0])
    sent(ysum.at[pl.ds(0, NY - 1)], y_s.at[0])
    pltpu.make_async_copy(pv, prolong, p_sem.at[0]).wait()


def shards(a_tiles, modes, col_tiles, fetch_list):
    fetch = jnp.pad(fetch_list, ((0, 0), (0, LIST - GHOSTS)))
    cols = jnp.pad(col_tiles, ((0, 0), (0, SLOTP - SLOTS)), constant_values=-1).reshape(1, TILE_DEV * SLOTP)
    dma = pltpu.SemaphoreType.DMA
    vmem = pl.BlockSpec(memory_space=pltpu.VMEM)
    smem = pl.BlockSpec(memory_space=pltpu.SMEM)
    hbm = pl.BlockSpec(memory_space=pl.ANY)
    plane = NX * NY
    one = dma((1,))
    prolong, coarse = pl.pallas_call(
        body,
        out_shape=(
            jax.ShapeDtypeStruct((TILE_DEV, SLOTS, MODES, ROWS), BF),
            jax.ShapeDtypeStruct((GROUP, MODES * MODES), F32),
        ),
        in_specs=[vmem, vmem, smem, smem, vmem, hbm],
        out_specs=(hbm, vmem),
        scratch_shapes=[
            pltpu.VMEM((TILE_DEV, SLOTS, ROWS, ROWS), BF),
            pltpu.VMEM((TILE_DEV * MODES, ROWS), F32),
            pltpu.VMEM((MODES, TILE_DEV, ROWS), BF),
            pltpu.VMEM((NZ, NC, NX, NY, TILE_DEV, ROWS), BF),
            pltpu.VMEM((TILES, ROWS), F32),
            pltpu.VMEM((plane, 1, LIST), jnp.int32),
            pltpu.SMEM((plane, 1, LIST), jnp.int32),
            pltpu.VMEM((GHOSTP, ROWS), F32),
            pltpu.VMEM((plane, GHOSTP, ROWS), BF),
            pltpu.VMEM((plane, GHOSTP, ROWS), BF),
            pltpu.VMEM((plane * GHOSTP, ROWS), F32),
            pltpu.VMEM((GROUP + GHOSTS, MODES, ROWS), BF),
            pltpu.VMEM((TILE_DEV, SLOTS, MODES, ROWS), BF),
            pltpu.VMEM((SLOTS, MODES, ROWS), BF),
            pltpu.VMEM((TILE_DEV * SLOTP, MODES * MODES), BF),
            pltpu.VMEM((OUT_ROWS, TILE_DEV * SLOTP), BF),
            pltpu.VMEM((8, 128), jnp.int32),
            pltpu.VMEM((NZ, 8, 128), jnp.int32),
            pltpu.VMEM((NX * NC, NZ, 8, 128), jnp.int32),
            pltpu.VMEM((128, GROUPS * 8), BF),
            pltpu.VMEM((NZ, NX * NC, 8, MODES * MODES), BF),
            pltpu.VMEM((NZ, NX * NC, 8, MODES * MODES), BF),
            pltpu.VMEM((NX * NC, NZ, 8, MODES * MODES), BF),
            pltpu.VMEM((NY, GROUP, MODES * MODES), BF),
            dma((TILE_DEV,)),
            one, dma((NX,)),
            one, one,
            dma((3,)),
            one, one,
            one, dma((2, NZ // 2, NQ)),
            one, dma((2, NZ // 2 + 1, NQ)),
            one, one,
            one, one, one, one,
            one, one, one, one,
            one, one,
            one,
        ],
        compiler_params=pltpu.CompilerParams(
            collective_id=0, has_side_effects=True, vmem_limit_bytes=56 * 2**20
        ),
    )(modes, fetch, fetch, cols, cols, a_tiles)
    return prolong, coarse


def solution(mesh):
    in_specs = (
        P(("sub", "blk"), None, None, None),
        P(("sub", "blk"), None, None),
        P(("sub", "blk"), None),
        P(("sub", "blk"), None),
    )
    out_specs = (P(("sub", "blk"), None, None, None), P("sub", None))
    return jax.shard_map(shards, mesh=mesh, in_specs=in_specs, out_specs=out_specs, check_vma=False)
```

time: 123 us -> 89.2 us (0.73)
  Pallas kernels: 0 us -> 82.5 us
  waiting for transfers between devices: 39.9 us -> 0 us
  starting transfers between devices: 31.8 us -> 0 us
  blocking collectives: 20.1 us -> 0 us
  matrix products: 10.9 us -> 0 us
  local copies, waits for them, and re-layouts: 15.6 us -> 5.84 us
  other arithmetic: 3.94 us -> 0 us
    pallas_call x0 -> x1, Pallas kernels: none -> 82.5 us  [shards(): pl.pallas_call(body, out_shape=(jax.ShapeDtypeStruct((TILE_DEV, SLOTS, MO...]
    all_to_all x3 -> x0, waiting for transfers between devices: 39.9 us -> none  [the longest x1 26.8 us: shards(): lax.all_to_all(picked, 'sub', split_axis=0, concat_axis=0, tiled=True)]
    all_to_all x3 -> x0, starting transfers between devices: 31.8 us -> none  [the longest x1 13 us: shards(): lax.all_to_all(requests, 'sub', split_axis=0, concat_axis=0, tiled=True)]
    all_gather x1 -> x0, blocking collectives: 11.2 us -> none  [shards(): group_modes = lax.all_gather(modes, 'blk', axis=0, tiled=True)]
    dot_general x5 -> x0, matrix products: 10.9 us -> none  [the longest x1 7.47 us: shards(): jnp.einsum('tkrc,tkmc->tkmr', a_tiles, gathered, preferred_element_type=j...]
    all_to_all x1 -> x0, blocking collectives: 8.94 us -> none  [sent_to_all(): return lax.all_to_all(copies, axis, split_axis=0, concat_axis=0, tiled=True)]
    gather x5 -> x0, local copies, waits for them, and re-layouts: 6.35 us -> none  [the longest x2 2.01 us: shards(): jnp.diagonal(a_tiles[:, 0], axis1=1, axis2=2).astype(jnp.float32)]
    select_n x3 -> x0, other arithmetic: 1.49 us -> none  [the longest x1 1.36 us: shards(): jnp.where(present[:, :, None, None], picked, jnp.zeros_like(picked))]
  transfers between devices with their start and end apart: 3 -> 0, of which waited for: 2 -> 0; matrix products, arithmetic and copies ran while one was open for 5% -> 0% of each run, Pallas kernels for 0% -> 0%
where the time goes in v1:
time: 89.2 us; the launch traced here: 89 us
  Pallas kernels  82.5 us (92%)
  local copies, waits for them, and re-layouts  5.84 us (7%)
    pallas_call x1, Pallas kernels, shards(): pl.pallas_call(body, out_shape=(jax.ShapeDtypeStruct((TILE_DEV, SLOTS, MO...  82.5 us
    unnamed x5, local copies, waits for them, and re-layouts  3.94 us

profile of v1, /device:TPU:1, one launch (start us, length us, event | category | flops | bytes accessed | tf_op | source)
XLA Modules:
  0.0 89.0 jit_solution(10130143701566145359)
XLA Ops:
  0.6 1.2 %pad.8.fetch_v.fetch_s = s32[1,256]{1,0:T(1,128)} pad(s32[1,130]{1,0:T(1,128)} %param.7, s32[]{:T(128)} %constant.0.clone.1), padding=0_0x0_126 | pad | bytes 1548 | tf_op jit(solution)/shard_map/jit(_pad)/pad | solution.py:312
  1.9 0.8 copy.8
  2.7 0.6 reshape.7.col_s.col_v
  3.3 82.5 %shard_map.59 = (bf16[24,12,16,128]{3,2,1,0:T(8,128)(2,1)}, f32[96,256]{1,0:T(8,128)}) custom-call(bf16[24,16,128]{2,1,0:T(8,128)(2,1)} %modes.1, s32[1,256]{1,0:T(1,128)} %pad.8.fetch_v.fetch_s, s32[1,256]{1,0:T(1,128)} %pad.8.fetch_v.fetch_s, s32[1,384]{1,0:T(1,128)} %reshape.7.col_s.col_v, s32[1,384]{1,0:T(1,128)} %reshape.7.col_s.col_v, ...), custom_call_target="tpu_custom_call" | custom-call | tf_op jit(solution)/shard_map/pallas_call | solution.py:320
  85.9 0.0 copy-start
  85.9 2.5 %copy.11 = bf16[24,12,16,128]{3,2,1,0:T(8,128)(2,1)} copy(bf16[24,12,16,128]{3,2,1,0:T(8,128)(2,1)} %get-tuple-element.4) | data formatting | bytes 2359296
  88.4 0.0 copy-done
  88.4 0.6 copy.12
  (1 shorter events, 0.0 us)
Async XLA Ops:
  85.9 2.5 %copy-start = (f32[96,256]{1,0:T(8,128)S(1)}, f32[96,256]{1,0:T(8,128)}, u32[]{:S(2)}) copy-start(f32[96,256]{1,0:T(8,128)} %get-tuple-element.5) | copy-start | bytes 294916

commit v2 on v1

--- a/solution.py
+++ b/solution.py
@@ -14,6 +14,7 @@
 TILE_DEV = 24
 SLOTS = 12
 SLOTP = 16
+TP = 32
 ROWS = 128
 MODES = 16
 GROUP = 96
@@ -23,7 +24,7 @@
 GHOSTS = 130
 GHOSTP = 144
 LIST = 256
-NQ = 2
+NQ = 4
 XQ = NX // NQ
 OUT_ROWS = GROUP + GROUPS * 8
 DAMPING = 2.0 / 3.0
@@ -44,11 +45,11 @@
 
 
 def body(
-    modes, fetch_v, fetch_s, col_s, col_v, a_hbm, prolong, coarse,
-    a_v, mf, s1, blocks, rows_f, lists_v, lists_s, stage, msg, got, got_f, table,
-    pv, qv, flat, seg, req, idx1, idx2, target, out, in1, in2, ysum,
+    modes, fetch_in, fetch_s, col_s, col_v, a_hbm, prolong, coarse,
+    fetch_v, col_f, a_v, mf, s1, blocks, rows_f, lists_v, lists_s, stage, msg, got, got_f, table,
+    pv, qv, flat, seg, req, idx1, idx2, target, out, back, ysum,
     a_sem, scat_s, scat_r, list_s, list_r, own_sem, all_s, all_r, ring_s, ring_r, sib_s, sib_r,
-    ex_s, ex_r, id1_s, id1_r, id2_s, id2_r, c1_s, c1_r, c2_s, c2_r, y_s, y_r, p_sem,
+    ex_s, ex_r, id1_s, id1_r, id2_s, id2_r, c1_s, c1_r, y_s, y_r, p_sem,
 ):
     s = lax.axis_index("sub")
     y = lax.axis_index("blk")
@@ -73,9 +74,6 @@
     def along_y(d):
         return dev(z, x, c, lax.rem(y + d, NY))
 
-    for t in range(TILE_DEV):
-        pltpu.make_async_copy(a_hbm.at[t], a_v.at[t], a_sem.at[t]).start()
-
     barrier = pltpu.get_barrier_semaphore()
     partners = [plane(p)[1] for p in range(1, NX * NY)]
     partners += [along_z(d)[1] for d in range(1, NZ)]
@@ -92,6 +90,8 @@
     request = jnp.full((8, 128), -1, jnp.int32)
     slots = col_v[...]
     colvec = slots
+    fetch_v[...] = jnp.zeros((1, LIST), jnp.int32)
+    fetch_v[:, :GHOSTS] = fetch_in[...]
     for h in range(GHOSTS):
         tile = fetch_s[0, h]
         group = tile // GROUP
@@ -100,6 +100,17 @@
         )
         slots = jnp.where(colvec == GROUP + h, GROUP + group * 8 + h % PER_PEER, slots)
     req[...] = request
+    col_f[...] = jnp.full((SLOTP, 128), -1, jnp.int32)
+    col_f[:SLOTS, :TILE_DEV] = slots
+    lane1 = lax.broadcasted_iota(jnp.int32, (1, 128), 1)
+    rows = []
+    for k0 in range(0, SLOTS, 4):
+        row = col_f[k0 : k0 + 1, :]
+        for j in range(1, 4):
+            row = jnp.where(lane1 // TP == j, pltpu.roll(col_f[k0 + j : k0 + j + 1, :], TP * j, 1), row)
+        rows.append(row)
+    slots = jnp.concatenate(rows, axis=1)
+    flat[...] = jnp.zeros((2 * SLOTS * TP, 128), F32)
 
     pl.semaphore_wait(barrier, len(partners))
 
@@ -107,6 +118,41 @@
     for p in range(1, NX * NY):
         t, device = plane(p)
         rcopy(s1.at[t], blocks.at[z, c, x, y], scat_s.at[0], scat_r.at[x], device).start()
+    def piece(k, core, q):
+        return blocks.at[k, core, pl.ds(q * XQ, XQ)]
+
+    def ring(way, step, q, k):
+        part = piece(k, c, q)
+        device = right if way == 0 else left
+        rcopy(part, part, ring_s.at[0], ring_r.at[way, step, q], device).start()
+
+    def pass_on(way, step, q, k):
+        part = piece(k, c, q)
+        rcopy(part, part, sib_s.at[0], sib_r.at[way, step, q], sibling).start()
+
+    def widen(k, core, q):
+        for i in range(XQ * NY):
+            xs, ys = q * XQ + i // NY, i % NY
+            base = ((k * NX + xs) * NC + core) * GROUP + ys * TILE_DEV
+            rows_f[pl.ds(pl.multiple_of(base, 8), TILE_DEV), :] = blocks[k, core, xs, ys].astype(F32)
+
+    def from_sibling(way, step, q, k):
+        part = piece(k, 1 - c, q)
+        rcopy(part, part, sib_s.at[0], sib_r.at[way, step, q], sibling).wait_recv()
+        widen(k, 1 - c, q)
+
+    last = NZ // 2
+    for q in range(NQ):
+        for xs in range(q * XQ, (q + 1) * XQ):
+            part = blocks.at[z, c, xs]
+            rcopy(part, part, scat_s.at[0], scat_r.at[xs], sibling).wait_recv()
+        ring(0, 0, q, z)
+        ring(1, 0, q, z)
+        pass_on(0, 0, q, z)
+
+    for t in range(TILE_DEV):
+        pltpu.make_async_copy(a_hbm.at[t], a_v.at[t], a_sem.at[t]).start()
+
     pltpu.make_async_copy(fetch_v, lists_v.at[me], own_sem.at[0]).start()
     for p in range(1, NX * NY):
         rcopy(fetch_v, lists_v.at[me], list_s.at[0], list_r.at[0], plane(p)[1]).start()
@@ -118,67 +164,38 @@
         rcopy(modes, mine, all_s.at[0], all_r.at[0], along_y(d)).start()
     idx1[z] = request
 
-    def piece(k, core, q):
-        return blocks.at[k, core, pl.ds(q * XQ, XQ)]
-
-    def ring(way, step, q, k):
-        part = piece(k, c, q)
-        device = right if way == 0 else left
-        rcopy(part, part, ring_s.at[0], ring_r.at[way, step, q], device).start()
-
-    def pass_on(way, step, q, k):
-        part = piece(k, c, q)
-        rcopy(part, part, sib_s.at[0], sib_r.at[way, step, q], sibling).start()
-
-    def widen(k, core, q):
-        @pl.loop(0, XQ * NY)
-        def _(i):
-            xs, ys = q * XQ + i // NY, lax.rem(i, NY)
-            base = ((k * NX + xs) * NC + core) * GROUP + ys * TILE_DEV
-            rows_f[pl.ds(pl.multiple_of(base, 8), TILE_DEV), :] = blocks[k, core, xs, ys].astype(F32)
-
-    def from_sibling(way, step, q, k):
-        part = piece(k, 1 - c, q)
-        rcopy(part, part, sib_s.at[0], sib_r.at[way, step, q], sibling).wait_recv()
-        widen(k, 1 - c, q)
-
-    last = NZ // 2
-    for q in range(NQ):
-        for xs in range(q * XQ, (q + 1) * XQ):
-            part = blocks.at[z, c, xs]
-            rcopy(part, part, scat_s.at[0], scat_r.at[xs], sibling).wait_recv()
-        ring(0, 0, q, z)
-        ring(1, 0, q, z)
-        pass_on(0, 0, q, z)
-
-    pltpu.make_async_copy(fetch_v, lists_v.at[me], own_sem.at[0]).wait()
-    others = lists_v.at[pl.ds(0, NX * NY - 1)]
-    rcopy(others, others, list_s.at[0], list_r.at[0], sibling).wait_recv()
-    pltpu.make_async_copy(lists_v, lists_s, own_sem.at[2]).start()
-    others = idx1.at[pl.ds(0, NZ - 1)]
-    rcopy(others, others, id1_s.at[0], id1_r.at[0], sibling).wait_recv()
-    for d in range(1, NX * NC):
-        rcopy(idx1, idx2.at[xc], id2_s.at[0], id2_r.at[0], across(d)[1]).start()
-    idx2[xc] = idx1[...]
     for q in range(NQ):
         widen(z, c, q)
+
+    def side_two():
+        pltpu.make_async_copy(fetch_v, lists_v.at[me], own_sem.at[0]).wait()
+        others = lists_v.at[pl.ds(0, NX * NY - 1)]
+        rcopy(others, others, list_s.at[0], list_r.at[0], sibling).wait_recv()
+        pltpu.make_async_copy(lists_v, lists_s, own_sem.at[2]).start()
+        others = idx1.at[pl.ds(0, NZ - 1)]
+        rcopy(others, others, id1_s.at[0], id1_r.at[0], sibling).wait_recv()
+        for d in range(1, NX * NC):
+            rcopy(idx1, idx2.at[xc], id2_s.at[0], id2_r.at[0], across(d)[1]).start()
+        idx2[xc] = idx1[...]
 
     events = []
     for step in range(1, last + 1):
         for q in range(NQ):
             for way in range(2):
-                if step < last or q == way:
+                if step < last or q * 2 // NQ == way:
                     events.append((way, step, q))
     pending = [(0, 0, q, z) for q in range(NQ)]
     for way, step, q in events:
         k = lax.rem(z + NZ - step, NZ) if way == 0 else lax.rem(z + step, NZ)
         part = piece(k, c, q)
         rcopy(part, part, ring_s.at[0], ring_r.at[way, step - 1, q], sibling).wait_recv()
-        if step < last - 1 or (step == last - 1 and q == way):
+        if step < last - 1 or (step == last - 1 and q * 2 // NQ == way):
             ring(way, step, q, k)
         pass_on(way, step, q, k)
         widen(k, c, q)
         pending.append((way, step, q, k))
+        if (way, step, q) == (1, 2, NQ - 1):
+            side_two()
         if len(pending) > 3:
             from_sibling(*pending.pop(0))
     pltpu.make_async_copy(lists_v, lists_s, own_sem.at[2]).wait()
@@ -201,11 +218,11 @@
 
     got[me] = pick(me)
 
-    place = lax.broadcasted_iota(jnp.int32, (OUT_ROWS, TILE_DEV * SLOTP), 0)
+    place = lax.broadcasted_iota(jnp.int32, (OUT_ROWS, SLOTS * TP), 0)
     seg[...] = (place == slots).astype(F32).astype(BF)
     others = idx2.at[pl.ds(0, NX * NC - 1)]
     rcopy(others, others, id2_s.at[0], id2_r.at[0], sibling).wait_recv()
-    wanted = idx2[...].reshape(GROUPS * 8, 128)
+    wanted = jnp.concatenate([idx2[g % (NX * NC), g // (NX * NC)] for g in range(GROUPS)], axis=0)
     lanes = lax.broadcasted_iota(jnp.int32, (GROUPS * 8, 128), 1)
     chosen = jnp.sum(jnp.where(lanes == s, wanted, 0).astype(F32), axis=1, keepdims=True)
     target[...] = (lanes.astype(F32) == chosen).astype(F32).T.astype(BF)
@@ -241,45 +258,60 @@
         == lax.broadcasted_iota(jnp.int32, (SLOTP, n), 1) // MODES
     ).astype(F32).astype(BF)
 
-    @pl.loop(0, TILE_DEV)
-    def _(t):
+    def products(t):
         pltpu.make_async_copy(a_hbm.at[t], a_v.at[t], a_sem.at[t]).wait()
         diagonal = jnp.sum(jnp.where(eye, a_v[t, 0].astype(F32), 0.0), axis=0, keepdims=True)
         scale = DAMPING / diagonal
-        for k in range(SLOTS):
-            column = table[col_s[0, t * SLOTP + k]]
-            product = dot_t(column, a_v[t, k])
-            value = -scale * product
-            if k == 0:
-                value = modes[t].astype(F32) + value
-            pv[t, k] = value.astype(BF)
-            qv[k] = product.astype(BF)
-        both = dot_t(pv[t].reshape(n, ROWS), qv[...].reshape(n, ROWS)) * (1.0 / ROWS)
-        both = jnp.where(same_slot, both, 0.0).astype(BF)
+        for k in range(0, SLOTS, 2):
+            columns = jnp.concatenate([table[col_s[k, t]], table[col_s[k + 1, t]]], axis=0)
+            two = dot_t(columns, a_v[t, pl.ds(k, 2)].reshape(2 * ROWS, ROWS))
+            parts = [two[:MODES, :ROWS], two[MODES:, ROWS:]]
+            for j, product in enumerate(parts):
+                value = -scale * product
+                if k + j == 0:
+                    value = modes[t].astype(F32) + value
+                pv[t, k + j] = value.astype(BF)
+                qv[t, k + j] = product.astype(BF)
+
+    def pairs(t):
+        both = dot_t(pv[t].reshape(n, ROWS), qv[t].reshape(n, ROWS)) * (1.0 / ROWS)
+        return jnp.where(same_slot, both, 0.0).astype(BF)
+
+    def widened(both):
         wide = jnp.dot(both, spread, preferred_element_type=F32)
-        wide = jnp.where(same_mode, wide, 0.0).astype(BF)
-        flat[pl.ds(pl.multiple_of(t * SLOTP, SLOTP), SLOTP), :] = jnp.dot(
-            fold, wide, preferred_element_type=F32
-        ).astype(BF)
+        return jnp.where(same_mode, wide, 0.0)
+
+    def folded(t, wide):
+        res = jnp.dot(fold, wide.astype(BF), preferred_element_type=F32)
+        flat[pl.ds(t, SLOTS, stride=TP), :] = res[:SLOTS, :128]
+        flat[pl.ds(SLOTS * TP + t, SLOTS, stride=TP), :] = res[:SLOTS, 128:]
+
+    @pl.loop(0, TILE_DEV, step=4)
+    def _(t0):
+        for u in range(4):
+            products(t0 + u)
+
+        bs = [pairs(t0 + u) for u in range(4)]
+        ws = [widened(v) for v in bs]
+        for u in range(4):
+            folded(t0 + u, ws[u])
 
     pltpu.make_async_copy(pv, prolong, p_sem.at[0]).start()
 
-    sums = jnp.dot(seg[...], flat[...], preferred_element_type=F32)
-    out[...] = sums[GROUP:].astype(BF).reshape(NZ, NX * NC, 8, MODES * MODES)
-    for d in range(1, NZ):
-        tz, device = along_z(d)
-        rcopy(out.at[tz], in1.at[z], c1_s.at[0], c1_r.at[0], device).start()
-    in1[z] = out[z]
-    others = in1.at[pl.ds(0, NZ - 1)]
+    terms = jnp.concatenate([flat[: SLOTS * TP, :], flat[SLOTS * TP :, :]], axis=1).astype(BF)
+    sums = jnp.dot(seg[...], terms, preferred_element_type=F32)
+    out[...] = sums[GROUP:].astype(BF).reshape(GROUPS, 8, MODES * MODES)
+
+    @pl.loop(1, GROUPS)
+    def _(d):
+        t = lax.rem(s + d, GROUPS)
+        rcopy(out.at[t], back.at[s], c1_s.at[0], c1_r.at[0], (t, y)).start()
+
+    back[s] = out[s]
+    others = back.at[pl.ds(0, GROUPS - 1)]
     rcopy(others, others, c1_s.at[0], c1_r.at[0], sibling).wait_recv()
-    for d in range(1, NX * NC):
-        t, device = across(d)
-        rcopy(in1.at[:, t], in2.at[xc], c2_s.at[0], c2_r.at[0], device).start()
-    in2[xc] = in1[:, xc]
-    others = in2.at[pl.ds(0, NX * NC - 1)]
-    rcopy(others, others, c2_s.at[0], c2_r.at[0], sibling).wait_recv()
     returned = jnp.dot(
-        target[...], in2[...].reshape(GROUPS * 8, MODES * MODES), preferred_element_type=F32
+        target[...], back[...].reshape(GROUPS * 8, MODES * MODES), preferred_element_type=F32
     )
     ysum[y] = (sums[:GROUP] + returned[:GROUP]).astype(BF)
     for d in range(1, NY):
@@ -302,15 +334,13 @@
     sent(blocks.at[pl.ds(0, NZ - 1), c], ring_s.at[0])
     sent(blocks.at[:, c], sib_s.at[0])
     sent(msg.at[pl.ds(0, NX * NY - 1)], ex_s.at[0])
-    sent(out.at[pl.ds(0, NZ - 1)], c1_s.at[0])
-    sent(in2.at[pl.ds(0, NX * NC - 1)], c2_s.at[0])
+    sent(back.at[pl.ds(0, GROUPS - 1)], c1_s.at[0])
     sent(ysum.at[pl.ds(0, NY - 1)], y_s.at[0])
     pltpu.make_async_copy(pv, prolong, p_sem.at[0]).wait()
 
 
 def shards(a_tiles, modes, col_tiles, fetch_list):
-    fetch = jnp.pad(fetch_list, ((0, 0), (0, LIST - GHOSTS)))
-    cols = jnp.pad(col_tiles, ((0, 0), (0, SLOTP - SLOTS)), constant_values=-1).reshape(1, TILE_DEV * SLOTP)
+    cols = col_tiles.T
     dma = pltpu.SemaphoreType.DMA
     vmem = pl.BlockSpec(memory_space=pltpu.VMEM)
     smem = pl.BlockSpec(memory_space=pltpu.SMEM)
@@ -326,6 +356,8 @@
         in_specs=[vmem, vmem, smem, smem, vmem, hbm],
         out_specs=(hbm, vmem),
         scratch_shapes=[
+            pltpu.VMEM((1, LIST), jnp.int32),
+            pltpu.VMEM((SLOTP, 128), jnp.int32),
             pltpu.VMEM((TILE_DEV, SLOTS, ROWS, ROWS), BF),
             pltpu.VMEM((TILE_DEV * MODES, ROWS), F32),
             pltpu.VMEM((MODES, TILE_DEV, ROWS), BF),
@@ -339,16 +371,15 @@
             pltpu.VMEM((plane * GHOSTP, ROWS), F32),
             pltpu.VMEM((GROUP + GHOSTS, MODES, ROWS), BF),
             pltpu.VMEM((TILE_DEV, SLOTS, MODES, ROWS), BF),
-            pltpu.VMEM((SLOTS, MODES, ROWS), BF),
-            pltpu.VMEM((TILE_DEV * SLOTP, MODES * MODES), BF),
-            pltpu.VMEM((OUT_ROWS, TILE_DEV * SLOTP), BF),
+            pltpu.VMEM((TILE_DEV, SLOTS, MODES, ROWS), BF),
+            pltpu.VMEM((2 * SLOTS * TP, 128), F32),
+            pltpu.VMEM((OUT_ROWS, SLOTS * TP), BF),
             pltpu.VMEM((8, 128), jnp.int32),
             pltpu.VMEM((NZ, 8, 128), jnp.int32),
             pltpu.VMEM((NX * NC, NZ, 8, 128), jnp.int32),
             pltpu.VMEM((128, GROUPS * 8), BF),
-            pltpu.VMEM((NZ, NX * NC, 8, MODES * MODES), BF),
-            pltpu.VMEM((NZ, NX * NC, 8, MODES * MODES), BF),
-            pltpu.VMEM((NX * NC, NZ, 8, MODES * MODES), BF),
+            pltpu.VMEM((GROUPS, 8, MODES * MODES), BF),
+            pltpu.VMEM((GROUPS, 8, MODES * MODES), BF),
             pltpu.VMEM((NY, GROUP, MODES * MODES), BF),
             dma((TILE_DEV,)),
             one, dma((NX,)),
@@ -359,14 +390,14 @@
             one, dma((2, NZ // 2 + 1, NQ)),
             one, one,
             one, one, one, one,
-            one, one, one, one,
+            one, one,
             one, one,
             one,
         ],
         compiler_params=pltpu.CompilerParams(
             collective_id=0, has_side_effects=True, vmem_limit_bytes=56 * 2**20
         ),
-    )(modes, fetch, fetch, cols, cols, a_tiles)
+    )(modes, fetch_list, fetch_list, cols, cols, a_tiles)
     return prolong, coarse
 
 

time: 89.2 us -> 70.8 us (0.79)
  Pallas kernels: 82.5 us -> 66.9 us
  local copies, waits for them, and re-layouts: 5.84 us -> 3.17 us
    pallas_call x1, Pallas kernels: 82.5 us -> 66.9 us  [shards(): pl.pallas_call(body, out_shape=(jax.ShapeDtypeStruct((TILE_DEV, SLOTS, MO...]
    pad x2 -> x0, local copies, waits for them, and re-layouts: 1.25 us -> none  [the longest x1 1.25 us: shards(): fetch = jnp.pad(fetch_list, ((0, 0), (0, LIST - GHOSTS)))]
    unnamed x5 -> x4, local copies, waits for them, and re-layouts: 3.94 us -> 3.17 us
where the time goes in v2:
time: 70.8 us; the launch traced here: 70.7 us
  Pallas kernels  66.9 us (94%)
  local copies, waits for them, and re-layouts  3.17 us (4%)
    pallas_call x1, Pallas kernels, shards(): pl.pallas_call(body, out_shape=(jax.ShapeDtypeStruct((TILE_DEV, SLOTS, MO...  66.9 us
    unnamed x4, local copies, waits for them, and re-layouts  3.17 us

profile of v2, /device:TPU:1, one launch (start us, length us, event | category | flops | bytes accessed | tf_op | source)
XLA Modules:
  0.0 70.7 jit_solution(8476907414244428715)
XLA Ops:
  0.6 66.9 %shard_map.59 = (bf16[24,12,16,128]{3,2,1,0:T(8,128)(2,1)}, f32[96,256]{1,0:T(8,128)}) custom-call(bf16[24,16,128]{2,1,0:T(8,128)(2,1)} %modes.1, s32[1,130]{1,0:T(1,128)} %fetch_s.1, s32[1,130]{1,0:T(1,128)} %fetch_s.1, s32[12,24]{1,0:T(8,128)} %bitcast.1, s32[12,24]{1,0:T(8,128)} %bitcast.2, bf16[24,12,128,128]{3,2,1,0:T(8,128)(2,1)} %a_hbm.1), custom_call_target="tpu_custom_call" | custom-call | tf_op jit(solution)/shard_map/pallas_call | solution.py:350
  67.5 0.0 copy-start
  67.5 2.5 %copy.8 = bf16[24,12,16,128]{3,2,1,0:T(8,128)(2,1)} copy(bf16[24,12,16,128]{3,2,1,0:T(8,128)(2,1)} %get-tuple-element.4) | data formatting | bytes 2359296
  70.1 0.0 copy-done
  70.1 0.6 copy.9
Async XLA Ops:
  67.5 2.5 %copy-start = (f32[96,256]{1,0:T(8,128)S(1)}, f32[96,256]{1,0:T(8,128)}, u32[]{:S(2)}) copy-start(f32[96,256]{1,0:T(8,128)} %get-tuple-element.5) | copy-start | bytes 294916

commit v3 on v2

--- a/solution.py
+++ b/solution.py
@@ -24,6 +24,8 @@
 GHOSTS = 130
 GHOSTP = 144
 LIST = 256
+PARTS = 4
+TOGETHER = 6
 NQ = 4
 XQ = NX // NQ
 OUT_ROWS = GROUP + GROUPS * 8
@@ -47,7 +49,7 @@
 def body(
     modes, fetch_in, fetch_s, col_s, col_v, a_hbm, prolong, coarse,
     fetch_v, col_f, a_v, mf, s1, blocks, rows_f, lists_v, lists_s, stage, msg, got, got_f, table,
-    pv, qv, flat, seg, req, idx1, idx2, target, out, back, ysum,
+    pv, qv, flat, seg, req, idx1, idx2, target, out, back, ysum, scales,
     a_sem, scat_s, scat_r, list_s, list_r, own_sem, all_s, all_r, ring_s, ring_r, sib_s, sib_r,
     ex_s, ex_r, id1_s, id1_r, id2_s, id2_r, c1_s, c1_r, y_s, y_r, p_sem,
 ):
@@ -115,8 +117,8 @@
     pl.semaphore_wait(barrier, len(partners))
 
     pltpu.make_async_copy(s1.at[me], blocks.at[z, c, x, y], scat_r.at[x]).start()
-    for p in range(1, NX * NY):
-        t, device = plane(p)
+    for i in range(1, NX * NY):
+        t, device = plane(i * 7 % (NX * NY))
         rcopy(s1.at[t], blocks.at[z, c, x, y], scat_s.at[0], scat_r.at[x], device).start()
     def piece(k, core, q):
         return blocks.at[k, core, pl.ds(q * XQ, XQ)]
@@ -210,7 +212,8 @@
     stage[pl.ds(GHOSTS - 2, GHOSTP - GHOSTS + 2), :] = jnp.zeros((GHOSTP - GHOSTS + 2, ROWS), F32)
 
     @pl.loop(1, NX * NY)
-    def _(p):
+    def _(i):
+        p = lax.rem(i * 7, NX * NY)
         tx, ty = lax.rem(x + p // NY, NX), lax.rem(y + lax.rem(p, NY), NY)
         t = tx * NY + ty
         msg[t] = pick(t)
@@ -226,6 +229,18 @@
     lanes = lax.broadcasted_iota(jnp.int32, (GROUPS * 8, 128), 1)
     chosen = jnp.sum(jnp.where(lanes == s, wanted, 0).astype(F32), axis=1, keepdims=True)
     target[...] = (lanes.astype(F32) == chosen).astype(F32).T.astype(BF)
+
+    eye = lax.broadcasted_iota(jnp.int32, (ROWS, ROWS), 0) == lax.broadcasted_iota(
+        jnp.int32, (ROWS, ROWS), 1
+    )
+
+    @pl.loop(0, TILE_DEV, step=4)
+    def _(t0):
+        for t in range(4):
+            pltpu.make_async_copy(a_hbm.at[t0 + t], a_v.at[t0 + t], a_sem.at[t0 + t]).wait()
+        for t in range(4):
+            diagonal = jnp.sum(jnp.where(eye, a_v[t0 + t, 0].astype(F32), 0.0), axis=0, keepdims=True)
+            scales[t0 + t] = DAMPING / diagonal
 
     pltpu.make_async_copy(modes, mine, own_sem.at[1]).wait()
     others = table.at[pl.ds(0, (NY - 1) * TILE_DEV)]
@@ -237,9 +252,6 @@
     for h in range(GHOSTS):
         table[GROUP + h] = got_f[pl.ds(h, MODES, stride=GHOSTP), :].astype(BF)
 
-    eye = lax.broadcasted_iota(jnp.int32, (ROWS, ROWS), 0) == lax.broadcasted_iota(
-        jnp.int32, (ROWS, ROWS), 1
-    )
     n = SLOTS * MODES
     same_slot = (
         lax.broadcasted_iota(jnp.int32, (n, n), 0) // MODES
@@ -259,9 +271,7 @@
     ).astype(F32).astype(BF)
 
     def products(t):
-        pltpu.make_async_copy(a_hbm.at[t], a_v.at[t], a_sem.at[t]).wait()
-        diagonal = jnp.sum(jnp.where(eye, a_v[t, 0].astype(F32), 0.0), axis=0, keepdims=True)
-        scale = DAMPING / diagonal
+        scale = scales[t]
         for k in range(0, SLOTS, 2):
             columns = jnp.concatenate([table[col_s[k, t]], table[col_s[k + 1, t]]], axis=0)
             two = dot_t(columns, a_v[t, pl.ds(k, 2)].reshape(2 * ROWS, ROWS))
@@ -286,14 +296,14 @@
         flat[pl.ds(t, SLOTS, stride=TP), :] = res[:SLOTS, :128]
         flat[pl.ds(SLOTS * TP + t, SLOTS, stride=TP), :] = res[:SLOTS, 128:]
 
-    @pl.loop(0, TILE_DEV, step=4)
+    @pl.loop(0, TILE_DEV, step=TOGETHER)
     def _(t0):
-        for u in range(4):
+        for u in range(TOGETHER):
             products(t0 + u)
 
-        bs = [pairs(t0 + u) for u in range(4)]
+        bs = [pairs(t0 + u) for u in range(TOGETHER)]
         ws = [widened(v) for v in bs]
-        for u in range(4):
+        for u in range(TOGETHER):
             folded(t0 + u, ws[u])
 
     pltpu.make_async_copy(pv, prolong, p_sem.at[0]).start()
@@ -304,7 +314,7 @@
 
     @pl.loop(1, GROUPS)
     def _(d):
-        t = lax.rem(s + d, GROUPS)
+        t = lax.rem(s + d * 37, GROUPS)
         rcopy(out.at[t], back.at[s], c1_s.at[0], c1_r.at[0], (t, y)).start()
 
     back[s] = out[s]
@@ -339,6 +349,25 @@
     pltpu.make_async_copy(pv, prolong, p_sem.at[0]).wait()
 
 
+def settle(prolong_in, coarse_in, prolong, coarse, held, held_c, in_s, out_s):
+    def parts(i):
+        if i == PARTS:
+            return coarse_in, held_c, coarse
+        span = pl.ds(i * (TILE_DEV // PARTS), TILE_DEV // PARTS)
+        return prolong_in.at[span], held.at[span], prolong.at[span]
+
+    for i in range(PARTS + 1):
+        src, mid, _ = parts(i)
+        pltpu.make_async_copy(src, mid, in_s.at[i]).start()
+    for i in range(PARTS + 1):
+        src, mid, dst = parts(i)
+        pltpu.make_async_copy(src, mid, in_s.at[i]).wait()
+        pltpu.make_async_copy(mid, dst, out_s.at[i]).start()
+    for i in range(PARTS + 1):
+        _, mid, dst = parts(i)
+        pltpu.make_async_copy(mid, dst, out_s.at[i]).wait()
+
+
 def shards(a_tiles, modes, col_tiles, fetch_list):
     cols = col_tiles.T
     dma = pltpu.SemaphoreType.DMA
@@ -347,12 +376,13 @@
     hbm = pl.BlockSpec(memory_space=pl.ANY)
     plane = NX * NY
     one = dma((1,))
+    shapes = (
+        jax.ShapeDtypeStruct((TILE_DEV, SLOTS, MODES, ROWS), BF),
+        jax.ShapeDtypeStruct((GROUP, MODES * MODES), F32),
+    )
     prolong, coarse = pl.pallas_call(
         body,
-        out_shape=(
-            jax.ShapeDtypeStruct((TILE_DEV, SLOTS, MODES, ROWS), BF),
-            jax.ShapeDtypeStruct((GROUP, MODES * MODES), F32),
-        ),
+        out_shape=shapes,
         in_specs=[vmem, vmem, smem, smem, vmem, hbm],
         out_specs=(hbm, vmem),
         scratch_shapes=[
@@ -381,6 +411,7 @@
             pltpu.VMEM((GROUPS, 8, MODES * MODES), BF),
             pltpu.VMEM((GROUPS, 8, MODES * MODES), BF),
             pltpu.VMEM((NY, GROUP, MODES * MODES), BF),
+            pltpu.VMEM((TILE_DEV, 1, ROWS), F32),
             dma((TILE_DEV,)),
             one, dma((NX,)),
             one, one,
@@ -398,7 +429,18 @@
             collective_id=0, has_side_effects=True, vmem_limit_bytes=56 * 2**20
         ),
     )(modes, fetch_list, fetch_list, cols, cols, a_tiles)
-    return prolong, coarse
+    return pl.pallas_call(
+        settle,
+        out_shape=shapes,
+        in_specs=[hbm, hbm],
+        out_specs=(hbm, hbm),
+        scratch_shapes=[
+            pltpu.VMEM((TILE_DEV, SLOTS, MODES, ROWS), BF),
+            pltpu.VMEM((GROUP, MODES * MODES), F32),
+            dma((PARTS + 1,)),
+            dma((PARTS + 1,)),
+        ],
+    )(prolong, coarse)
 
 
 def solution(mesh):

time: 70.8 us -> 65.4 us (0.924)
  local copies, waits for them, and re-layouts: 3.17 us -> 0 us
  Pallas kernels: 66.9 us -> 64.7 us
    unnamed x4 -> x0, local copies, waits for them, and re-layouts: 3.17 us -> none
    pallas_call x1 -> x2, Pallas kernels: 66.9 us -> 64.7 us  [the longest x1 62.6 us: shards(): pl.pallas_call(body, out_shape=shapes, in_specs=[vmem, vmem, smem, smem,...]
where the time goes in v3:
time: 65.4 us; the launch traced here: 65.3 us
  Pallas kernels  64.7 us (99%)
    pallas_call x1, Pallas kernels, shards(): pl.pallas_call(body, out_shape=shapes, in_specs=[vmem, vmem, smem, smem,...  62.6 us
    pallas_call x1, Pallas kernels, shards(): pl.pallas_call(settle, out_shape=shapes, in_specs=[hbm, hbm], out_specs=(...  2.08 us

profile of v3, /device:TPU:1, one launch (start us, length us, event | category | flops | bytes accessed | tf_op | source)
XLA Modules:
  0.0 65.3 jit_solution(9359072821302468691)
XLA Ops:
  0.6 62.6 %shard_map.59 = (bf16[24,12,16,128]{3,2,1,0:T(8,128)(2,1)}, f32[96,256]{1,0:T(8,128)}) custom-call(bf16[24,16,128]{2,1,0:T(8,128)(2,1)} %modes.1, s32[1,130]{1,0:T(1,128)} %fetch_s.1, s32[1,130]{1,0:T(1,128)} %fetch_s.1, s32[12,24]{1,0:T(8,128)} %bitcast.1, s32[12,24]{1,0:T(8,128)} %bitcast.2, bf16[24,12,128,128]{3,2,1,0:T(8,128)(2,1)} %a_hbm.1), custom_call_target="tpu_custom_call" | custom-call | tf_op jit(solution)/shard_map/pallas_call | solution.py:383
  63.2 2.1 %shard_map.60 = (bf16[24,12,16,128]{3,2,1,0:T(8,128)(2,1)}, f32[96,256]{1,0:T(8,128)}) custom-call(bf16[24,12,16,128]{3,2,1,0:T(8,128)(2,1)} %get-tuple-element.4.prolong_in, f32[96,256]{1,0:T(8,128)} %get-tuple-element.5.coarse_in), custom_call_target="tpu_custom_call" | custom-call | tf_op jit(solution)/shard_map/pallas_call | solution.py:432

commit v4 on v3

--- a/solution.py
+++ b/solution.py
@@ -27,7 +27,8 @@
 PARTS = 4
 TOGETHER = 6
 NQ = 4
-XQ = NX // NQ
+PLANE = NX * NY
+PQ = PLANE // NQ
 OUT_ROWS = GROUP + GROUPS * 8
 DAMPING = 2.0 / 3.0
 
@@ -49,7 +50,7 @@
 def body(
     modes, fetch_in, fetch_s, col_s, col_v, a_hbm, prolong, coarse,
     fetch_v, col_f, a_v, mf, s1, blocks, rows_f, lists_v, lists_s, stage, msg, got, got_f, table,
-    pv, qv, flat, seg, req, idx1, idx2, target, out, back, ysum, scales,
+    pv, qv, flat, seg, req, idx1, idx2, target, out, back, pack, unpack, ysum, scales,
     a_sem, scat_s, scat_r, list_s, list_r, own_sem, all_s, all_r, ring_s, ring_r, sib_s, sib_r,
     ex_s, ex_r, id1_s, id1_r, id2_s, id2_r, c1_s, c1_r, y_s, y_r, p_sem,
 ):
@@ -61,9 +62,9 @@
     right, left = dev(lax.rem(z + 1, NZ), x, c, y), dev(lax.rem(z + NZ - 1, NZ), x, c, y)
     sibling = dev(z, x, 1 - c, y)
 
-    def plane(p):
+    def plane(p, d=0):
         tx, ty = lax.rem(x + p // NY, NX), lax.rem(y + p % NY, NY)
-        return tx * NY + ty, dev(z, tx, c, ty)
+        return tx * NY + ty, dev(lax.rem(z + d, NZ), tx, c, ty)
 
     def along_z(d):
         tz = lax.rem(z + d, NZ)
@@ -77,8 +78,8 @@
         return dev(z, x, c, lax.rem(y + d, NY))
 
     barrier = pltpu.get_barrier_semaphore()
-    partners = [plane(p)[1] for p in range(1, NX * NY)]
-    partners += [along_z(d)[1] for d in range(1, NZ)]
+    partners = [plane(p, d)[1] for d in (0, 1, NZ - 1) for p in range(PLANE) if p or d]
+    partners += [along_z(d)[1] for d in range(2, NZ - 1)]
     partners += [dev(z, lax.rem(x + d, NX), 1 - c, y) for d in range(NX)]
     for partner in partners:
         pl.semaphore_signal(barrier, inc=1, device_id=partner, device_id_type=MESH)
@@ -86,6 +87,56 @@
     mf[...] = modes[...].astype(F32).reshape(TILE_DEV * MODES, ROWS)
     for m in range(MODES):
         s1[m] = mf[pl.ds(m, TILE_DEV, stride=MODES), :].astype(BF)
+
+    pl.semaphore_wait(barrier, len(partners))
+
+    pltpu.make_async_copy(s1.at[me], blocks.at[z, c, me], scat_r.at[0, me // PQ]).start()
+    for i in range(PLANE):
+        for j, d in ((1, 1), (2, NZ - 1), (0, 0)):
+            if i or d:
+                t, device = plane(i * 7 % PLANE, d)
+                rcopy(s1.at[t], blocks.at[z, c, me], scat_s.at[j], scat_r.at[j, me // PQ], device).start()
+
+    def piece(k, core, q):
+        return blocks.at[k, core, pl.ds(q * PQ, PQ)]
+
+    def ring(way, step, q, k):
+        part = piece(k, c, q)
+        device = right if way == 0 else left
+        rcopy(part, part, ring_s.at[0], ring_r.at[way, step - 1, q], device).start()
+
+    def pass_on(way, step, q, k):
+        part = piece(k, c, q)
+        rcopy(part, part, sib_s.at[0], sib_r.at[way, step, q], sibling).start()
+
+    def widen(k, core, q):
+        for u in range(q * PQ, (q + 1) * PQ):
+            base = ((k * NX + u // NY) * NC + core) * GROUP + u % NY * TILE_DEV
+            rows_f[pl.ds(pl.multiple_of(base, 8), TILE_DEV), :] = blocks[k, core, u].astype(F32)
+
+    def from_sibling(way, step, q, k):
+        part = piece(k, 1 - c, q)
+        rcopy(part, part, sib_s.at[0], sib_r.at[way, step, q], sibling).wait_recv()
+        widen(k, 1 - c, q)
+
+    last = NZ // 2
+
+    def arrived(j, q, k):
+        part = piece(k, c, q)
+        rcopy(part, part, scat_s.at[0], scat_r.at[j, q], sibling).wait_recv()
+
+    for q in range(NQ):
+        for way in range(2):
+            k = lax.rem(z + (NZ - 1, 1)[way], NZ)
+            arrived(1 + way, q, k)
+            ring(way, 1, q, k)
+            pass_on(way, 1, q, k)
+    for q in range(NQ):
+        arrived(0, q, z)
+        pass_on(0, 0, q, z)
+
+    for t in range(TILE_DEV):
+        pltpu.make_async_copy(a_hbm.at[t], a_v.at[t], a_sem.at[t]).start()
 
     lane = lax.broadcasted_iota(jnp.int32, (8, 128), 1)
     sub8 = lax.broadcasted_iota(jnp.int32, (8, 128), 0)
@@ -114,47 +165,6 @@
     slots = jnp.concatenate(rows, axis=1)
     flat[...] = jnp.zeros((2 * SLOTS * TP, 128), F32)
 
-    pl.semaphore_wait(barrier, len(partners))
-
-    pltpu.make_async_copy(s1.at[me], blocks.at[z, c, x, y], scat_r.at[x]).start()
-    for i in range(1, NX * NY):
-        t, device = plane(i * 7 % (NX * NY))
-        rcopy(s1.at[t], blocks.at[z, c, x, y], scat_s.at[0], scat_r.at[x], device).start()
-    def piece(k, core, q):
-        return blocks.at[k, core, pl.ds(q * XQ, XQ)]
-
-    def ring(way, step, q, k):
-        part = piece(k, c, q)
-        device = right if way == 0 else left
-        rcopy(part, part, ring_s.at[0], ring_r.at[way, step, q], device).start()
-
-    def pass_on(way, step, q, k):
-        part = piece(k, c, q)
-        rcopy(part, part, sib_s.at[0], sib_r.at[way, step, q], sibling).start()
-
-    def widen(k, core, q):
-        for i in range(XQ * NY):
-            xs, ys = q * XQ + i // NY, i % NY
-            base = ((k * NX + xs) * NC + core) * GROUP + ys * TILE_DEV
-            rows_f[pl.ds(pl.multiple_of(base, 8), TILE_DEV), :] = blocks[k, core, xs, ys].astype(F32)
-
-    def from_sibling(way, step, q, k):
-        part = piece(k, 1 - c, q)
-        rcopy(part, part, sib_s.at[0], sib_r.at[way, step, q], sibling).wait_recv()
-        widen(k, 1 - c, q)
-
-    last = NZ // 2
-    for q in range(NQ):
-        for xs in range(q * XQ, (q + 1) * XQ):
-            part = blocks.at[z, c, xs]
-            rcopy(part, part, scat_s.at[0], scat_r.at[xs], sibling).wait_recv()
-        ring(0, 0, q, z)
-        ring(1, 0, q, z)
-        pass_on(0, 0, q, z)
-
-    for t in range(TILE_DEV):
-        pltpu.make_async_copy(a_hbm.at[t], a_v.at[t], a_sem.at[t]).start()
-
     pltpu.make_async_copy(fetch_v, lists_v.at[me], own_sem.at[0]).start()
     for p in range(1, NX * NY):
         rcopy(fetch_v, lists_v.at[me], list_s.at[0], list_r.at[0], plane(p)[1]).start()
@@ -181,16 +191,21 @@
         idx2[xc] = idx1[...]
 
     events = []
-    for step in range(1, last + 1):
+    for step in range(2, last + 1):
         for q in range(NQ):
             for way in range(2):
                 if step < last or q * 2 // NQ == way:
                     events.append((way, step, q))
     pending = [(0, 0, q, z) for q in range(NQ)]
+    for q in range(NQ):
+        for way in range(2):
+            k = lax.rem(z + (NZ - 1, 1)[way], NZ)
+            widen(k, c, q)
+            pending.append((way, 1, q, k))
     for way, step, q in events:
         k = lax.rem(z + NZ - step, NZ) if way == 0 else lax.rem(z + step, NZ)
         part = piece(k, c, q)
-        rcopy(part, part, ring_s.at[0], ring_r.at[way, step - 1, q], sibling).wait_recv()
+        rcopy(part, part, ring_s.at[0], ring_r.at[way, step - 2, q], sibling).wait_recv()
         if step < last - 1 or (step == last - 1 and q * 2 // NQ == way):
             ring(way, step, q, k)
         pass_on(way, step, q, k)
@@ -198,8 +213,9 @@
         pending.append((way, step, q, k))
         if (way, step, q) == (1, 2, NQ - 1):
             side_two()
-        if len(pending) > 3:
-            from_sibling(*pending.pop(0))
+        for _ in range(2):
+            if len(pending) > 3:
+                from_sibling(*pending.pop(0))
     pltpu.make_async_copy(lists_v, lists_s, own_sem.at[2]).wait()
     for item in pending:
         from_sibling(*item)
@@ -229,6 +245,22 @@
     lanes = lax.broadcasted_iota(jnp.int32, (GROUPS * 8, 128), 1)
     chosen = jnp.sum(jnp.where(lanes == s, wanted, 0).astype(F32), axis=1, keepdims=True)
     target[...] = (lanes.astype(F32) == chosen).astype(F32).T.astype(BF)
+
+    full = MODES * MODES
+
+    def pair(entry):
+        m, n = entry // MODES, lax.rem(entry, MODES)
+        high, low = jnp.maximum(m, n), jnp.minimum(m, n)
+        return high * (high + 1) // 2 + low, m >= n
+
+    def lane_pair(at):
+        return jnp.where(at < 128, at, 128 + lax.rem(at, 8))
+
+    down = lax.broadcasted_iota(jnp.int32, (full, full), 0)
+    over = lax.broadcasted_iota(jnp.int32, (full, full), 1)
+    index, kept = pair(down)
+    pack[...] = ((index == lane_pair(over)) & kept).astype(F32).astype(BF)
+    unpack[...] = (pair(over)[0] == lane_pair(down)).astype(F32).astype(BF)
 
     eye = lax.broadcasted_iota(jnp.int32, (ROWS, ROWS), 0) == lax.broadcasted_iota(
         jnp.int32, (ROWS, ROWS), 1
@@ -310,7 +342,12 @@
 
     terms = jnp.concatenate([flat[: SLOTS * TP, :], flat[SLOTS * TP :, :]], axis=1).astype(BF)
     sums = jnp.dot(seg[...], terms, preferred_element_type=F32)
-    out[...] = sums[GROUP:].astype(BF).reshape(GROUPS, 8, MODES * MODES)
+    packed = jnp.dot(sums[GROUP:].astype(BF), pack[...], preferred_element_type=F32)
+    slot_row = lax.broadcasted_iota(jnp.int32, (GROUPS, 8, 128), 1)
+    own_lanes = lax.broadcasted_iota(jnp.int32, (GROUPS, 8, 128), 2) // 8 == slot_row
+    rest = jnp.where(own_lanes, packed[:, 128:].reshape(GROUPS, 8, 128), 0.0)
+    rest = jnp.broadcast_to(jnp.sum(rest, axis=1, keepdims=True), (GROUPS, 8, 128))
+    out[...] = jnp.where(slot_row == PER_PEER, rest, packed[:, :128].reshape(GROUPS, 8, 128)).astype(BF)
 
     @pl.loop(1, GROUPS)
     def _(d):
@@ -320,9 +357,15 @@
     back[s] = out[s]
     others = back.at[pl.ds(0, GROUPS - 1)]
     rcopy(others, others, c1_s.at[0], c1_r.at[0], sibling).wait_recv()
-    returned = jnp.dot(
-        target[...], back[...].reshape(GROUPS * 8, MODES * MODES), preferred_element_type=F32
-    )
+    came = back[...]
+    rest = jnp.broadcast_to(came[:, PER_PEER : PER_PEER + 1, :].astype(F32), (GROUPS, 8, 128))
+    rest = jnp.where(own_lanes, rest, 0.0).astype(BF)
+    both = jnp.concatenate([came.reshape(GROUPS * 8, 128), rest.reshape(GROUPS * 8, 128)], axis=1)
+    found = jnp.dot(target[...], both, preferred_element_type=F32)
+    upper = found.astype(BF)
+    lower = (found - upper.astype(F32)).astype(BF)
+    returned = jnp.dot(upper, unpack[...], preferred_element_type=F32)
+    returned = returned + jnp.dot(lower, unpack[...], preferred_element_type=F32)
     ysum[y] = (sums[:GROUP] + returned[:GROUP]).astype(BF)
     for d in range(1, NY):
         rcopy(ysum.at[y], ysum.at[y], y_s.at[0], y_r.at[0], along_y(d)).start()
@@ -336,12 +379,14 @@
     def sent(region, sem):
         rcopy(region, region, sem, sem, sibling).wait_send()
 
-    sent(s1.at[pl.ds(0, NX * NY - 1)], scat_s.at[0])
+    sent(s1.at[pl.ds(0, PLANE - 1)], scat_s.at[0])
+    sent(s1, scat_s.at[1])
+    sent(s1, scat_s.at[2])
     sent(lists_v.at[pl.ds(0, NX * NY - 1)], list_s.at[0])
     sent(idx1.at[pl.ds(0, NZ - 1)], id1_s.at[0])
     sent(idx2.at[pl.ds(0, NX * NC - 1)], id2_s.at[0])
     sent(table.at[pl.ds(0, (NY - 1) * TILE_DEV)], all_s.at[0])
-    sent(blocks.at[pl.ds(0, NZ - 1), c], ring_s.at[0])
+    sent(blocks.at[pl.ds(0, NZ - 3), c], ring_s.at[0])
     sent(blocks.at[:, c], sib_s.at[0])
     sent(msg.at[pl.ds(0, NX * NY - 1)], ex_s.at[0])
     sent(back.at[pl.ds(0, GROUPS - 1)], c1_s.at[0])
@@ -391,7 +436,7 @@
             pltpu.VMEM((TILE_DEV, SLOTS, ROWS, ROWS), BF),
             pltpu.VMEM((TILE_DEV * MODES, ROWS), F32),
             pltpu.VMEM((MODES, TILE_DEV, ROWS), BF),
-            pltpu.VMEM((NZ, NC, NX, NY, TILE_DEV, ROWS), BF),
+            pltpu.VMEM((NZ, NC, PLANE, TILE_DEV, ROWS), BF),
             pltpu.VMEM((TILES, ROWS), F32),
             pltpu.VMEM((plane, 1, LIST), jnp.int32),
             pltpu.SMEM((plane, 1, LIST), jnp.int32),
@@ -408,16 +453,18 @@
             pltpu.VMEM((NZ, 8, 128), jnp.int32),
             pltpu.VMEM((NX * NC, NZ, 8, 128), jnp.int32),
             pltpu.VMEM((128, GROUPS * 8), BF),
-            pltpu.VMEM((GROUPS, 8, MODES * MODES), BF),
-            pltpu.VMEM((GROUPS, 8, MODES * MODES), BF),
+            pltpu.VMEM((GROUPS, 8, 128), BF),
+            pltpu.VMEM((GROUPS, 8, 128), BF),
+            pltpu.VMEM((MODES * MODES, MODES * MODES), BF),
+            pltpu.VMEM((MODES * MODES, MODES * MODES), BF),
             pltpu.VMEM((NY, GROUP, MODES * MODES), BF),
             pltpu.VMEM((TILE_DEV, 1, ROWS), F32),
             dma((TILE_DEV,)),
-            one, dma((NX,)),
+            dma((3,)), dma((3, NQ)),
             one, one,
             dma((3,)),
             one, one,
-            one, dma((2, NZ // 2, NQ)),
+            one, dma((2, NZ // 2 - 1, NQ)),
             one, dma((2, NZ // 2 + 1, NQ)),
             one, one,
             one, one, one, one,

time: 65.4 us -> 62.6 us (0.957)
  Pallas kernels: 64.7 us -> 61.8 us
    pallas_call x1, Pallas kernels: 62.6 us -> 59.7 us  [shards(): pl.pallas_call(body, out_shape=shapes, in_specs=[vmem, vmem, smem, smem,...]
where the time goes in v4:
time: 62.6 us; the launch traced here: 62.4 us
  Pallas kernels  61.8 us (99%)
  between operations  0.64 us (1%)
    pallas_call x1, Pallas kernels, shards(): pl.pallas_call(body, out_shape=shapes, in_specs=[vmem, vmem, smem, smem,...  59.7 us
    pallas_call x1, Pallas kernels, shards(): pl.pallas_call(settle, out_shape=shapes, in_specs=[hbm, hbm], out_specs=(...  2.08 us

profile of v4, /device:TPU:1, one launch (start us, length us, event | category | flops | bytes accessed | tf_op | source)
XLA Modules:
  0.0 62.4 jit_solution(12608505803743439029)
XLA Ops:
  0.6 59.7 %shard_map.59 = (bf16[24,12,16,128]{3,2,1,0:T(8,128)(2,1)}, f32[96,256]{1,0:T(8,128)}) custom-call(bf16[24,16,128]{2,1,0:T(8,128)(2,1)} %modes.1, s32[1,130]{1,0:T(1,128)} %fetch_s.1, s32[1,130]{1,0:T(1,128)} %fetch_s.1, s32[12,24]{1,0:T(8,128)} %bitcast.1, s32[12,24]{1,0:T(8,128)} %bitcast.2, bf16[24,12,128,128]{3,2,1,0:T(8,128)(2,1)} %a_hbm.1), custom_call_target="tpu_custom_call" | custom-call | tf_op jit(solution)/shard_map/pallas_call | solution.py:428
  60.4 2.1 %shard_map.60 = (bf16[24,12,16,128]{3,2,1,0:T(8,128)(2,1)}, f32[96,256]{1,0:T(8,128)}) custom-call(bf16[24,12,16,128]{3,2,1,0:T(8,128)(2,1)} %get-tuple-element.4.prolong_in, f32[96,256]{1,0:T(8,128)} %get-tuple-element.5.coarse_in), custom_call_target="tpu_custom_call" | custom-call | tf_op jit(solution)/shard_map/pallas_call | solution.py:479

commit v5 on v4

--- a/solution.py
+++ b/solution.py
@@ -163,7 +163,7 @@
             row = jnp.where(lane1 // TP == j, pltpu.roll(col_f[k0 + j : k0 + j + 1, :], TP * j, 1), row)
         rows.append(row)
     slots = jnp.concatenate(rows, axis=1)
-    flat[...] = jnp.zeros((2 * SLOTS * TP, 128), F32)
+    flat[...] = jnp.zeros((2 * SLOTS * TP + 4 * TP, 128), F32)
 
     pltpu.make_async_copy(fetch_v, lists_v.at[me], own_sem.at[0]).start()
     for p in range(1, NX * NY):
@@ -340,21 +340,22 @@
 
     pltpu.make_async_copy(pv, prolong, p_sem.at[0]).start()
 
-    terms = jnp.concatenate([flat[: SLOTS * TP, :], flat[SLOTS * TP :, :]], axis=1).astype(BF)
-    sums = jnp.dot(seg[...], terms, preferred_element_type=F32)
-    packed = jnp.dot(sums[GROUP:].astype(BF), pack[...], preferred_element_type=F32)
+    terms = jnp.concatenate([flat[: SLOTS * TP, :], flat[SLOTS * TP : 2 * SLOTS * TP, :]], axis=1).astype(BF)
+    remote = jnp.dot(seg[GROUP:, :], terms, preferred_element_type=F32)
+    packed = jnp.dot(remote.astype(BF), pack[...], preferred_element_type=F32)
     slot_row = lax.broadcasted_iota(jnp.int32, (GROUPS, 8, 128), 1)
     own_lanes = lax.broadcasted_iota(jnp.int32, (GROUPS, 8, 128), 2) // 8 == slot_row
     rest = jnp.where(own_lanes, packed[:, 128:].reshape(GROUPS, 8, 128), 0.0)
     rest = jnp.broadcast_to(jnp.sum(rest, axis=1, keepdims=True), (GROUPS, 8, 128))
     out[...] = jnp.where(slot_row == PER_PEER, rest, packed[:, :128].reshape(GROUPS, 8, 128)).astype(BF)
 
-    @pl.loop(1, GROUPS)
+    @pl.loop(1, GROUPS, unroll=7)
     def _(d):
         t = lax.rem(s + d * 37, GROUPS)
         rcopy(out.at[t], back.at[s], c1_s.at[0], c1_r.at[0], (t, y)).start()
 
     back[s] = out[s]
+    local = jnp.dot(seg[:GROUP, :], terms, preferred_element_type=F32)
     others = back.at[pl.ds(0, GROUPS - 1)]
     rcopy(others, others, c1_s.at[0], c1_r.at[0], sibling).wait_recv()
     came = back[...]
@@ -366,7 +367,7 @@
     lower = (found - upper.astype(F32)).astype(BF)
     returned = jnp.dot(upper, unpack[...], preferred_element_type=F32)
     returned = returned + jnp.dot(lower, unpack[...], preferred_element_type=F32)
-    ysum[y] = (sums[:GROUP] + returned[:GROUP]).astype(BF)
+    ysum[y] = (local + returned[:GROUP]).astype(BF)
     for d in range(1, NY):
         rcopy(ysum.at[y], ysum.at[y], y_s.at[0], y_r.at[0], along_y(d)).start()
     others = ysum.at[pl.ds(0, NY - 1)]
@@ -437,7 +438,7 @@
             pltpu.VMEM((TILE_DEV * MODES, ROWS), F32),
             pltpu.VMEM((MODES, TILE_DEV, ROWS), BF),
             pltpu.VMEM((NZ, NC, PLANE, TILE_DEV, ROWS), BF),
-            pltpu.VMEM((TILES, ROWS), F32),
+            pltpu.VMEM((TILES + 8, ROWS), F32),
             pltpu.VMEM((plane, 1, LIST), jnp.int32),
             pltpu.SMEM((plane, 1, LIST), jnp.int32),
             pltpu.VMEM((GHOSTP, ROWS), F32),
@@ -447,7 +448,7 @@
             pltpu.VMEM((GROUP + GHOSTS, MODES, ROWS), BF),
             pltpu.VMEM((TILE_DEV, SLOTS, MODES, ROWS), BF),
             pltpu.VMEM((TILE_DEV, SLOTS, MODES, ROWS), BF),
-            pltpu.VMEM((2 * SLOTS * TP, 128), F32),
+            pltpu.VMEM((2 * SLOTS * TP + 4 * TP, 128), F32),
             pltpu.VMEM((OUT_ROWS, SLOTS * TP), BF),
             pltpu.VMEM((8, 128), jnp.int32),
             pltpu.VMEM((NZ, 8, 128), jnp.int32),

time: 62.6 us -> 62.5 us (level)
  no operation moved by 1% of the time
where the time goes in v5:
time: 62.5 us; the launch traced here: 62.3 us
  Pallas kernels  61.7 us (99%)
  between operations  0.64 us (1%)
    pallas_call x1, Pallas kernels, shards(): pl.pallas_call(body, out_shape=shapes, in_specs=[vmem, vmem, smem, smem,...  59.6 us
    pallas_call x1, Pallas kernels, shards(): pl.pallas_call(settle, out_shape=shapes, in_specs=[hbm, hbm], out_specs=(...  2.08 us

profile of v5, /device:TPU:1, one launch (start us, length us, event | category | flops | bytes accessed | tf_op | source)
XLA Modules:
  0.0 62.3 jit_solution(10198557722553605449)
XLA Ops:
  0.6 59.6 %shard_map.59 = (bf16[24,12,16,128]{3,2,1,0:T(8,128)(2,1)}, f32[96,256]{1,0:T(8,128)}) custom-call(bf16[24,16,128]{2,1,0:T(8,128)(2,1)} %modes.1, s32[1,130]{1,0:T(1,128)} %fetch_s.1, s32[1,130]{1,0:T(1,128)} %fetch_s.1, s32[12,24]{1,0:T(8,128)} %bitcast.1, s32[12,24]{1,0:T(8,128)} %bitcast.2, bf16[24,12,128,128]{3,2,1,0:T(8,128)(2,1)} %a_hbm.1), custom_call_target="tpu_custom_call" | custom-call | tf_op jit(solution)/shard_map/pallas_call | solution.py:429
  60.3 2.1 %shard_map.60 = (bf16[24,12,16,128]{3,2,1,0:T(8,128)(2,1)}, f32[96,256]{1,0:T(8,128)}) custom-call(bf16[24,12,16,128]{3,2,1,0:T(8,128)(2,1)} %get-tuple-element.4.prolong_in, f32[96,256]{1,0:T(8,128)} %get-tuple-element.5.coarse_in), custom_call_target="tpu_custom_call" | custom-call | tf_op jit(solution)/shard_map/pallas_call | solution.py:480

commit v6 on v5

--- a/solution.py
+++ b/solution.py
@@ -25,7 +25,7 @@
 GHOSTP = 144
 LIST = 256
 PARTS = 4
-TOGETHER = 6
+TOGETHER = 8
 NQ = 4
 PLANE = NX * NY
 PQ = PLANE // NQ
@@ -80,7 +80,7 @@
     barrier = pltpu.get_barrier_semaphore()
     partners = [plane(p, d)[1] for d in (0, 1, NZ - 1) for p in range(PLANE) if p or d]
     partners += [along_z(d)[1] for d in range(2, NZ - 1)]
-    partners += [dev(z, lax.rem(x + d, NX), 1 - c, y) for d in range(NX)]
+    partners.append(sibling)
     for partner in partners:
         pl.semaphore_signal(barrier, inc=1, device_id=partner, device_id_type=MESH)
 

time: 62.5 us -> 62.2 us (level)
  no operation moved by 1% of the time
where the time goes in v6:
time: 62.2 us; the launch traced here: 62 us
  Pallas kernels  61.4 us (99%)
  between operations  0.64 us (1%)
    pallas_call x1, Pallas kernels, shards(): pl.pallas_call(body, out_shape=shapes, in_specs=[vmem, vmem, smem, smem,...  59.3 us
    pallas_call x1, Pallas kernels, shards(): pl.pallas_call(settle, out_shape=shapes, in_specs=[hbm, hbm], out_specs=(...  2.08 us

profile of v6, /device:TPU:1, one launch (start us, length us, event | category | flops | bytes accessed | tf_op | source)
XLA Modules:
  0.0 62.0 jit_solution(7424295385278603699)
XLA Ops:
  0.6 59.3 %shard_map.59 = (bf16[24,12,16,128]{3,2,1,0:T(8,128)(2,1)}, f32[96,256]{1,0:T(8,128)}) custom-call(bf16[24,16,128]{2,1,0:T(8,128)(2,1)} %modes.1, s32[1,130]{1,0:T(1,128)} %fetch_s.1, s32[1,130]{1,0:T(1,128)} %fetch_s.1, s32[12,24]{1,0:T(8,128)} %bitcast.1, s32[12,24]{1,0:T(8,128)} %bitcast.2, bf16[24,12,128,128]{3,2,1,0:T(8,128)(2,1)} %a_hbm.1), custom_call_target="tpu_custom_call" | custom-call | tf_op jit(solution)/shard_map/pallas_call | solution.py:429
  59.9 2.1 %shard_map.60 = (bf16[24,12,16,128]{3,2,1,0:T(8,128)(2,1)}, f32[96,256]{1,0:T(8,128)}) custom-call(bf16[24,12,16,128]{3,2,1,0:T(8,128)(2,1)} %get-tuple-element.4.prolong_in, f32[96,256]{1,0:T(8,128)} %get-tuple-element.5.coarse_in), custom_call_target="tpu_custom_call" | custom-call | tf_op jit(solution)/shard_map/pallas_call | solution.py:480
